TPU v7x, 32 devices: a whole 2x2x4 slice. The times are simulated.
32 devices in a mesh: blk: 16 (over z, y, core), grp: 2 (over x).
Axes of the slice: x: 2, y: 2, z: 4, core: 2. Of those that a mesh axis runs over, the one named last changes fastest.
Arguments:
- entities: float32 [32768, 400], P('blk'), may hold values from -3 to 3
- relations: float32 [64, 400], replicated, may hold values from -1.8 to 1.8
- head_row: int32 [12288], P(('blk', 'grp')), may hold values from 0 to 2047
- relation_id: int32 [12288], P(('blk', 'grp')), may hold values from 0 to 63
- tail_owner: int32 [12288, 1], P(('blk', 'grp')), may hold values from 0 to 15; in each aligned block of 384 rows (0 to 383, 384 to 767, ...) at most 48 rows name the same one
- tail_row: int32 [12288], P(('blk', 'grp')), may hold values from 0 to 2047
- negative_rows: int32 [16, 64], P('blk'), may hold values from 0 to 2047
- edge_count: int32 [32], P(('blk', 'grp')), may hold values from 96 to 384, as said below
Outputs:
- new_entities: float32 [32768, 400], P('blk')
- new_relations: float32 [64, 400], replicated
Inputs may be any that keep to these rules, and one draw needn't show every extreme that they name: `tail_owner`: among the 384 edge slots of one device no partition is named more than 48 times, a bound that some block reaches. `edge_count`: some device has all 384 slots live.
All inputs are finite; a program needn't handle non-finite values.
Results may differ from a plain program's by a relative error of at most 0.0003.
The roundings to bfloat16 on the way count: a program that leaves them out, or rounds other values in their place, can miss the bound.
Values may be sent and summed in bfloat16 or wider, within the bound.
A program may use at most 128 MiB of HBM per device.

v0:
```python
import jax
import jax.numpy as jnp
from jax import lax
from jax.sharding import PartitionSpec as P

EPSILON = 1e-06
LEARN_RATE = 0.3


def complex_product(factor, other):
    half_width = factor.shape[1] // 2
    factor_real, factor_imag = (factor[:, :half_width], factor[:, half_width:])
    other_real, other_imag = (other[:, :half_width], other[:, half_width:])
    return jnp.concatenate(
        [
            factor_real * other_real - factor_imag * other_imag,
            factor_real * other_imag + factor_imag * other_real,
        ],
        axis=1,
    )


def complex_grads(upstream, head_vals, rel_vals):
    half_width = upstream.shape[1] // 2
    grad_real, grad_imag = (upstream[:, :half_width], upstream[:, half_width:])
    head_real, head_imag = (head_vals[:, :half_width], head_vals[:, half_width:])
    rel_real, rel_imag = (rel_vals[:, :half_width], rel_vals[:, half_width:])
    grad_head = jnp.concatenate(
        [grad_real * rel_real + grad_imag * rel_imag, grad_imag * rel_real - grad_real * rel_imag],
        axis=1,
    )
    grad_rel = jnp.concatenate(
        [
            grad_real * head_real + grad_imag * head_imag,
            grad_imag * head_real - grad_real * head_imag,
        ],
        axis=1,
    )
    return (grad_head, grad_rel)


def adagrad(table, table_grads):
    square_mean = jnp.mean(table_grads * table_grads, axis=1, keepdims=True)
    return table - LEARN_RATE * table_grads / (jnp.sqrt(square_mean) + EPSILON)


def per_device(
    entities, relations, head_row, relation_id, tail_owner, tail_row, negative_rows, edge_count
):
    owners = lax.axis_size("blk")
    edge_total = head_row.shape[0]
    row_width = entities.shape[1]
    neg_count = negative_rows.shape[1]
    rel_count = relations.shape[0]
    capacity = max(2, 2 * edge_total // owners)
    live = (jnp.arange(edge_total, dtype=jnp.int32) < edge_count[0]).astype(jnp.float32)
    head_bf = entities[head_row].astype(jnp.bfloat16)
    rel_onehot = (relation_id[:, None] == jnp.arange(rel_count, dtype=jnp.int32)[None, :]).astype(
        jnp.float32
    )
    rel_rows = jnp.dot(rel_onehot, relations, precision=lax.Precision.HIGHEST)
    query_bf = complex_product(head_bf.astype(jnp.float32), rel_rows).astype(jnp.bfloat16)
    target = tail_owner[:, 0]
    target_hot = (target[:, None] == jnp.arange(owners, dtype=jnp.int32)[None, :]).astype(jnp.int32)
    earlier = jnp.cumsum(target_hot, axis=0) - target_hot
    slot_index = jnp.sum(earlier * target_hot, axis=1)
    position = target * capacity + slot_index
    requests = (
        jnp.zeros((owners * capacity,), jnp.int32)
        .at[position]
        .set(tail_row)
        .reshape(owners, capacity)
    )
    requested = lax.all_to_all(requests, "blk", split_axis=0, concat_axis=0, tiled=True)
    located = entities[requested].astype(jnp.bfloat16)
    arrived = lax.all_to_all(located, "blk", split_axis=0, concat_axis=0, tiled=True)
    tail_bf = arrived.reshape(owners * capacity, row_width)[position]
    query_f = query_bf.astype(jnp.float32)
    positive = jnp.sum(query_f * tail_bf.astype(jnp.float32), axis=1)
    weight = -live * jax.nn.sigmoid(-positive)
    grad_tail = weight[:, None] * query_f
    outgoing = jnp.zeros((owners * capacity, row_width), jnp.float32).at[position].set(grad_tail)
    returned = lax.all_to_all(
        outgoing.reshape(owners, capacity, row_width),
        "blk",
        split_axis=0,
        concat_axis=0,
        tiled=True,
    )
    neg_scale = 1.0 / (owners * neg_count)
    own_block = entities[negative_rows[0]].astype(jnp.bfloat16)
    start_query = weight[:, None] * tail_bf.astype(jnp.float32)
    piece = lax.all_gather(own_block, "blk", axis=0, tiled=True)
    grad_query = start_query
    scores = jnp.dot(query_bf, piece.T, preferred_element_type=jnp.float32)
    nweight = (neg_scale * live[:, None] * jax.nn.sigmoid(scores)).astype(jnp.bfloat16)
    grad_query = grad_query + jnp.dot(nweight, piece, preferred_element_type=jnp.float32)
    block_grad = jnp.dot(nweight.T, query_bf, preferred_element_type=jnp.float32)
    neg_grads = block_grad
    grad_query, neg_grads = (grad_query, neg_grads)
    grad_head, grad_rel = complex_grads(grad_query, head_bf.astype(jnp.float32), rel_rows)
    entity_grads = jnp.zeros(entities.shape, jnp.float32)
    entity_grads = entity_grads.at[head_row].add(grad_head)
    entity_grads = entity_grads.at[requested.reshape(-1)].add(returned.reshape(-1, row_width))
    block_sum = lax.psum_scatter(neg_grads, "blk", scatter_dimension=0, tiled=True)
    entity_grads = entity_grads.at[negative_rows[0]].add(block_sum)
    rel_local = jnp.dot(rel_onehot.T, grad_rel, precision=lax.Precision.HIGHEST)
    rel_total = lax.psum(rel_local, ("blk", "grp"))
    new_relations = adagrad(relations, rel_total)
    summed = lax.psum(entity_grads, "grp")
    new_entities = adagrad(entities, summed)
    return (new_entities, new_relations)


def solution(mesh):
    return jax.shard_map(
        per_device,
        mesh=mesh,
        in_specs=(
            P("blk", None),
            P(),
            P(("blk", "grp")),
            P(("blk", "grp")),
            P(("blk", "grp"), None),
            P(("blk", "grp")),
            P("blk", None),
            P(("blk", "grp")),
        ),
        out_specs=(P("blk", None), P()),
        check_vma=False,
    )
```

profile of v0, /device:TPU:0, one launch (start us, length us, event | category | flops | bytes accessed | tf_op | source)
XLA Modules:
  0.0 373.3 jit_solution(12056419527415314321)
XLA Ops:
  8.0 0.7 reduce
  8.7 0.9 reduce-window.6
  9.6 0.2 slice_reduce_fusion
  9.8 0.1 fusion.16
  9.9 0.7 fusion.22
  10.6 3.1 scatter_custom_fusion
  13.7 0.7 all_to_all.14
  14.4 7.4 %all-to-all-start = ((s32[16,1,48]{2,1,0:T(1,128)}), s32[16,1,48]{2,1,0:T(1,128)S(1)}, u32[]{:S(2)}, u32[]{:S(2)}) async-start(s32[16,1,48]{2,1,0:T(1,128)} %all_to_all.14), calls=%async_computation | async-start | bytes 16384 | tf_op jit(solution)/shard_map/all_to_all | solution.py:74
  22.5 0.7 fusion.23
  23.1 0.7 compare_select_fusion.3
  23.8 0.6 copy-done.6
  24.4 5.0 %copy.23 = f32[2048,400]{1,0:T(8,128)} copy(f32[2048,400]{0,1:T(8,128)} %param.8) | data formatting | bytes 6553600 | tf_op args[0]
  29.4 4.3 %gather_fusion = bf16[384,400]{1,0:T(8,128)(2,1)S(1)} fusion(f32[2048,400]{1,0:T(8,128)} %copy.23, s32[1024]{0:T(1024)S(1)} %pad_clamp_fusion.3), kind=kCustom, calls=%fused_computation | custom fusion | bytes 615936 | tf_op jit(solution)/shard_map/gather | solution.py:57
  33.7 0.0 copy-done.8
  33.7 0.2 copy.16
  34.0 0.0 copy-done.3
  34.0 0.0 copy-done.5
  34.0 0.5 fusion.10
  34.6 0.1 subtract_convert_fusion
  34.7 2.9 gather_fusion.3
  37.6 0.0 all-to-all-done
  37.6 0.0 copy-start.4
  37.6 0.1 reshape.170
  37.7 5.5 %gather_fusion.1 = bf16[768,400]{1,0:T(8,128)(2,1)} fusion(f32[2048,400]{1,0:T(8,128)} %copy.23, s32[1024]{0:T(1024)S(1)} %pad_clamp_fusion.2), kind=kCustom, calls=%fused_computation.1 | custom fusion | bytes 1231872 | tf_op jit(solution)/shard_map/gather | solution.py:75
  43.2 0.0 copy-done.4
  43.2 6.0 %all-to-all-start.1 = ((bf16[16,48,400]{2,1,0:T(8,128)(2,1)}), bf16[16,48,400]{2,1,0:T(8,128)(2,1)S(1)}, u32[]{:S(2)}, u32[]{:S(2)}) async-start(bf16[16,48,400]{2,1,0:T(8,128)(2,1)} %bitcast.3), calls=%async_computation.1 | async-start | bytes 1572864 | tf_op jit(solution)/shard_map/all_to_all | solution.py:76
  49.3 0.0 reduce-scatter.2.cloned.1.call-start
  49.3 32.9 %all_gather.3 = bf16[1024,400]{1,0:T(8,128)(2,1)S(1)} all-gather(bf16[64,400]{1,0:T(8,128)(2,1)S(1)} %gather_fusion.3), channel_id=1, replica_groups=mesh['blk'=16,'grp'=2] {'blk'}, dimensions={0}, use_global_device_ids=true | all-gather | bytes 870400 | tf_op jit(solution)/shard_map/all_gather | solution.py:93
  82.3 0.8 multiply_convert_fusion
  83.1 0.2 copy-done.1
  83.2 2.1 fusion.25
  85.3 0.0 reduce-scatter.2.cloned.1.call-update
  85.4 0.0 all-to-all-done.1
  85.4 2.6 gather_fusion.2
  88.0 1.2 copy.19
  89.2 0.1 fusion.4
  89.3 0.1 convert_multiply_fusion.2
  89.4 0.3 copy.22
  89.6 3.2 scatter_custom_fusion.2
  92.8 4.4 %all-to-all-start.2 = ((f32[16,48,400]{2,1,0:T(8,128)}), f32[16,48,400]{2,1,0:T(8,128)S(1)}, u32[]{:S(2)}, u32[]{:S(2)}) async-start(f32[16,48,400]{2,1,0:T(8,128)} %bitcast.7), calls=%async_computation.2 | async-start | bytes 3145728 | tf_op jit(solution)/shard_map/all_to_all | solution.py:83
  97.3 0.0 all-reduce.5.cloned.1.call-start
  97.3 0.5 broadcast.187
  97.9 1.3 reduce.11
  99.2 0.1 reshape.157
  99.3 2.2 convolution_add_fusion
  101.5 0.1 multiply_add_fusion
  101.6 1.9 fusion.5
  103.5 0.0 all-reduce.5.cloned.1.call-update
  103.5 0.2 all-reduce.3.cloned.1.call-start
  103.8 0.3 copy.21
  104.1 5.2 %scatter_custom_fusion.1 = f32[2048,400]{1,0:T(8,128)} fusion(s32[384]{0:T(512)} %copy-done.6, f32[384,400]{1,0:T(8,128)S(1)} %copy.21, f32[]{:T(128)} %constant.10.clone.1), kind=kCustom, calls=%fused_computation.11 | custom fusion | flops 153600 | bytes 3277312 | tf_op jit(solution)/shard_map/scatter-add | solution.py:103
  109.2 28.5 %all-to-all-done.2 = f32[16,48,400]{2,1,0:T(8,128)S(1)} async-done(((f32[16,48,400]{2,1,0:T(8,128)}), f32[16,48,400]{2,1,0:T(8,128)S(1)}, u32[]{:S(2)}, u32[]{:S(2)}) %all-to-all-start.2) | async-done | bytes 1228832 | tf_op jit(solution)/shard_map/all_to_all | solution.py:83
  137.8 10.9 %scatter_fusion = f32[2048,400]{1,0:T(8,128)} fusion(f32[2048,400]{1,0:T(8,128)} %scatter_custom_fusion.1, s32[768]{0:T(1024)S(1)} %fusion.18, f32[768,400]{1,0:T(8,128)S(1)} %bitcast.43), kind=kCustom, calls=%fused_computation.7 | custom fusion | flops 307200 | bytes 3689472 | tf_op jit(solution)/shard_map/scatter-add | solution.py:104
  148.6 6.9 %reduce-scatter.2.cloned.1.call-done = f32[64,400]{1,0:T(8,128)} async-done(((f32[1024,400]{1,0:T(8,128)}), f32[64,400]{1,0:T(8,128)}) %reduce-scatter.2.cloned.1.call-update) | async-done | bytes 102416 | tf_op jit(solution)/shard_map/reduce_scatter | solution.py:105
  155.5 5.4 %scatter_fusion.1 = f32[2048,400]{1,0:T(8,128)} fusion(f32[2048,400]{1,0:T(8,128)} %scatter_fusion, s32[64]{0:T(128)S(1)} %copy-done.9, f32[64,400]{1,0:T(8,128)} %reduce-scatter.2.cloned.1.call-done), kind=kCustom, calls=%fused_computation.8 | custom fusion | flops 25600 | bytes 307456 | tf_op jit(solution)/shard_map/scatter-add | solution.py:106
  160.9 0.0 all-reduce.3.cloned.1.call-update
  161.0 82.3 %all-reduce.5.cloned.1.call-done = f32[64,400]{1,0:T(8,128)} async-done(((f32[64,400]{1,0:T(8,128)}), f32[64,400]{1,0:T(8,128)}) %all-reduce.5.cloned.1.call-update) | async-done | bytes 102416 | tf_op jit(solution)/shard_map/psum | solution.py:108
  243.2 1.0 multiply_reduce_fusion.1
  244.3 1.7 divide_subtract_fusion.1
  245.9 106.5 %all-reduce.3.cloned.1.call-done = f32[2048,400]{1,0:T(8,128)} async-done(((f32[2048,400]{1,0:T(8,128)}), f32[2048,400]{1,0:T(8,128)}) %all-reduce.3.cloned.1.call-update) | async-done | bytes 3276816 | tf_op jit(solution)/shard_map/psum | solution.py:110
  352.4 2.7 multiply_reduce_fusion
  355.1 0.7 copy-done
  355.8 4.8 %divide_subtract_fusion = f32[2048,400]{1,0:T(8,128)} fusion(f32[2048,400]{1,0:T(8,128)S(1)} %copy-done, f32[2048,400]{1,0:T(8,128)} %all-reduce.3.cloned.1.call-done, f32[2048]{0:T(1024)S(1)} %sqrt_add_fusion), kind=kLoop, calls=%fused_computation.9 | loop fusion | flops 2457600 | bytes 9838592 | tf_op jit(solution)/shard_map/sub | solution.py:44
  360.6 5.2 %copy.24 = f32[2048,400]{0,1:T(8,128)} copy(f32[2048,400]{1,0:T(8,128)} %divide_subtract_fusion) | data formatting | bytes 6553600
  (26 shorter events, 0.2 us)
Async XLA Ops:
  10.6 74.7 %copy-start.7 = (s32[384]{0:T(512)}, s32[384]{0:T(512)S(1)}, u32[]{:S(2)}) copy-start(s32[384]{0:T(512)S(1)} %fusion.22) | copy-start | bytes 4612
  14.4 23.2 %all-to-all-start = ((s32[16,1,48]{2,1,0:T(1,128)}), s32[16,1,48]{2,1,0:T(1,128)S(1)}, u32[]{:S(2)}, u32[]{:S(2)}) async-start(s32[16,1,48]{2,1,0:T(1,128)} %all_to_all.14), calls=%async_computation | async-start | bytes 16384 | tf_op jit(solution)/shard_map/all_to_all | solution.py:74
  23.1 10.6 %copy-start.8 = (s32[64]{0:T(128)}, s32[64]{0:T(128)S(1)}, u32[]{:S(2)}) copy-start(s32[64]{0:T(128)S(1)} %fusion.23) | copy-start | bytes 772
  23.8 0.6 copy-start.6
  29.4 4.6 %copy-start.3 = (f32[64,400]{1,0:T(8,128)S(1)}, f32[64,400]{1,0:T(8,128)}, u32[]{:S(2)}) copy-start(f32[64,400]{1,0:T(8,128)} %param.9) | copy-start | bytes 307204
  29.4 4.6 %copy-start.5 = (s32[384]{0:T(512)S(1)}, s32[384]{0:T(512)}, u32[]{:S(2)}) copy-start(s32[384]{0:T(512)} %param.11) | copy-start | bytes 4612
  37.6 5.7 %copy-start.4 = (s32[16,1,48]{2,1,0:T(1,128)}, s32[16,1,48]{2,1,0:T(1,128)S(1)}, u32[]{:S(2)}) copy-start(s32[16,1,48]{2,1,0:T(1,128)S(1)} %all-to-all-done) | copy-start | bytes 9220
  43.2 42.1 %all-to-all-start.1 = ((bf16[16,48,400]{2,1,0:T(8,128)(2,1)}), bf16[16,48,400]{2,1,0:T(8,128)(2,1)S(1)}, u32[]{:S(2)}, u32[]{:S(2)}) async-start(bf16[16,48,400]{2,1,0:T(8,128)(2,1)} %bitcast.3), calls=%async_computation.1 | async-start | bytes 1572864 | tf_op jit(solution)/shard_map/all_to_all | solution.py:76
  49.3 106.2 %reduce-scatter.2.cloned.1.call-start = ((), (), s32[]{:S(2)}) async-start(), calls=%async_computation.4 | async-start | bytes 2228224 | tf_op jit(solution)/shard_map/reduce_scatter | solution.py:105
  82.2 1.0 copy-start.1
  83.2 4.7 %copy-start.2 = (bf16[384,1024]{1,0:T(8,128)(2,1)}, bf16[384,1024]{1,0:T(8,128)(2,1)S(1)}, u32[]{:S(2)}) copy-start(bf16[384,1024]{1,0:T(8,128)(2,1)S(1)} %multiply_convert_fusion) | copy-start | bytes 2359300
  92.8 44.9 %all-to-all-start.2 = ((f32[16,48,400]{2,1,0:T(8,128)}), f32[16,48,400]{2,1,0:T(8,128)S(1)}, u32[]{:S(2)}, u32[]{:S(2)}) async-start(f32[16,48,400]{2,1,0:T(8,128)} %bitcast.7), calls=%async_computation.2 | async-start | bytes 3145728 | tf_op jit(solution)/shard_map/all_to_all | solution.py:83
  97.3 146.0 %all-reduce.5.cloned.1.call-start = ((), (), s32[]{:S(2)}) async-start(), calls=%async_computation.6 | async-start | bytes 262144 | tf_op jit(solution)/shard_map/psum | solution.py:108
  103.5 248.8 %all-reduce.3.cloned.1.call-start = ((), (), s32[]{:S(2)}) async-start(), calls=%async_computation.5 | async-start | bytes 8388608 | tf_op jit(solution)/shard_map/psum | solution.py:110
  137.8 17.7 %copy-start.9 = (s32[64]{0:T(128)S(1)}, s32[64]{0:T(128)}, u32[]{:S(2)}) copy-start(s32[64]{0:T(128)} %copy-done.8) | copy-start | bytes 772
  352.4 3.4 copy-start
Sparse Core Ops, SparseCore 0:
  85.5 69.9 reduce-scatter.1
Sparse Core Ops, SparseCore 1:
  103.9 139.3 all-reduce.4
  245.7 106.6 all-reduce.2
where the time goes:
time: 374 us; the launch traced here: 373 us
  waiting for transfers between devices  224 us (60%)
  other arithmetic  37.3 us (10%)
  local copies, waits for them, and re-layouts  36.8 us (10%)
  blocking collectives  32.9 us (9%)
  starting transfers between devices  18.1 us (5%)
  between operations  16.4 us (4%)
  matrix products  7.49 us (2%)
    psum x1, waiting for transfers between devices, per_device(): summed = lax.psum(entity_grads, 'grp')  106 us
    psum x1, waiting for transfers between devices, per_device(): rel_total = lax.psum(rel_local, ('blk', 'grp'))  82.3 us
    all_gather x1, blocking collectives, per_device(): piece = lax.all_gather(own_block, 'blk', axis=0, tiled=True)  32.9 us
    all_to_all x1, waiting for transfers between devices, per_device(): lax.all_to_all(outgoing.reshape(owners, capacity, row_width), 'blk', spli...  28.5 us
    unnamed x22, local copies, waits for them, and re-layouts  11.7 us
    scatter-add x1, other arithmetic, per_device(): entity_grads.at[requested.reshape(-1)].add(returned.reshape(-1, row_width))  10.9 us
  transfers between devices with their start and end apart: 6, of which 4 were waited for; matrix products, arithmetic and copies ran while one was open for 15% of the time, Pallas kernels for 0%

commit v1 on v0

v1 whole, which is shorter than its diff:
```python
import jax
import jax.numpy as jnp
from jax import lax
from jax.sharding import PartitionSpec as P

EPSILON = 1e-06
LEARN_RATE = 0.3
NEG_TYPE = jnp.bfloat16


def complex_product(factor, other):
    half_width = factor.shape[1] // 2
    factor_real, factor_imag = (factor[:, :half_width], factor[:, half_width:])
    other_real, other_imag = (other[:, :half_width], other[:, half_width:])
    return jnp.concatenate(
        [
            factor_real * other_real - factor_imag * other_imag,
            factor_real * other_imag + factor_imag * other_real,
        ],
        axis=1,
    )


def complex_grads(upstream, head_vals, rel_vals):
    half_width = upstream.shape[1] // 2
    grad_real, grad_imag = (upstream[:, :half_width], upstream[:, half_width:])
    head_real, head_imag = (head_vals[:, :half_width], head_vals[:, half_width:])
    rel_real, rel_imag = (rel_vals[:, :half_width], rel_vals[:, half_width:])
    grad_head = jnp.concatenate(
        [grad_real * rel_real + grad_imag * rel_imag, grad_imag * rel_real - grad_real * rel_imag],
        axis=1,
    )
    grad_rel = jnp.concatenate(
        [
            grad_real * head_real + grad_imag * head_imag,
            grad_imag * head_real - grad_real * head_imag,
        ],
        axis=1,
    )
    return (grad_head, grad_rel)


def adagrad(table, table_grads):
    square_mean = jnp.mean(table_grads * table_grads, axis=1, keepdims=True)
    return table - LEARN_RATE * table_grads / (jnp.sqrt(square_mean) + EPSILON)


def hot_rows(index, count, dtype):
    return (index[:, None] == jnp.arange(count, dtype=jnp.int32)[None, :]).astype(dtype)


def pick(hot, table):
    return jnp.dot(hot, table, preferred_element_type=jnp.float32).astype(jnp.bfloat16)


def spread(rows, count, grads):
    hot = hot_rows(rows, count, jnp.bfloat16)
    high = lax.reduce_precision(grads, 8, 7)
    both = jnp.concatenate([high, grads - high], axis=1).astype(jnp.bfloat16)
    sums = lax.dot_general(
        hot, both, (((0,), (0,)), ((), ())), preferred_element_type=jnp.float32
    )
    width = grads.shape[1]
    return sums[:, :width] + sums[:, width:]


def swap(own):
    pairs = [(i, (i + 1) % lax.axis_size("grp")) for i in range(lax.axis_size("grp"))]
    other = lax.ppermute(own, "grp", pairs)
    first = lax.axis_index("grp") == 0
    return jnp.concatenate([jnp.where(first, own, other), jnp.where(first, other, own)], axis=0)


def deal(blocks, axes):
    return lax.all_to_all(blocks, axes, split_axis=0, concat_axis=0, tiled=True)


def per_device(
    entities, relations, head_row, relation_id, tail_owner, tail_row, negative_rows, edge_count
):
    owners = lax.axis_size("blk")
    devices = owners * lax.axis_size("grp")
    edge_total = head_row.shape[0]
    ent_count, row_width = entities.shape
    neg_count = negative_rows.shape[1]
    rel_count = relations.shape[0]
    capacity = max(2, 2 * edge_total // owners)
    alive = jnp.arange(edge_total, dtype=jnp.int32) < edge_count[0]
    live = alive.astype(jnp.float32)
    target = tail_owner[:, 0]
    target_hot = hot_rows(target, owners, jnp.float32)
    order = jnp.arange(edge_total, dtype=jnp.int32)
    before = (order[:, None] > order[None, :]).astype(jnp.bfloat16)
    earlier = jnp.dot(before, target_hot.astype(jnp.bfloat16), preferred_element_type=jnp.float32)
    slot_index = jnp.sum(earlier * target_hot, axis=1).astype(jnp.int32)
    position = target * capacity + slot_index
    slot_hot = hot_rows(position, owners * capacity, jnp.bfloat16)
    wanted = jnp.where(alive, tail_row, -1)
    taken = hot_rows(position, owners * capacity, jnp.int32)
    requests = jnp.sum(taken * (wanted + 1)[:, None], axis=0) - 1
    requested = deal(requests.reshape(owners, capacity), "blk").reshape(-1)

    table = entities.astype(jnp.bfloat16)
    own_block = pick(hot_rows(negative_rows[0], ent_count, jnp.bfloat16), table)
    piece = lax.all_gather(own_block, "blk", axis=0, tiled=True)
    located = pick(hot_rows(requested, ent_count, jnp.bfloat16), table)
    arrived = deal(located.reshape(owners, capacity, row_width), "blk")

    head_bf = pick(hot_rows(head_row, ent_count, jnp.bfloat16), table)
    rel_onehot = hot_rows(relation_id, rel_count, jnp.float32)
    rel_rows = jnp.dot(rel_onehot, relations, precision=lax.Precision.HIGHEST)
    head_f = head_bf.astype(jnp.float32)
    query_bf = complex_product(head_f, rel_rows).astype(jnp.bfloat16)
    query_f = query_bf.astype(jnp.float32)
    outgoing = lax.dot_general(
        slot_hot, query_bf, (((0,), (0,)), ((), ())), preferred_element_type=jnp.float32
    ).astype(jnp.bfloat16)
    returned = deal(outgoing.reshape(owners, capacity, row_width), "blk").reshape(-1, row_width)

    neg_scale = 1.0 / (owners * neg_count)
    scores = jnp.dot(query_bf, piece.T, preferred_element_type=jnp.float32)
    nweight = (neg_scale * live[:, None] * jax.nn.sigmoid(scores)).astype(jnp.bfloat16)
    neg_query = jnp.dot(nweight, piece, preferred_element_type=jnp.float32)
    neg_grads = jnp.dot(nweight.T, query_bf, preferred_element_type=jnp.float32)
    neg_parts = deal(neg_grads.astype(NEG_TYPE).reshape(owners, neg_count, row_width), "blk")
    neg_sum = jnp.sum(neg_parts.astype(jnp.float32), axis=0)

    tail_bf = pick(slot_hot, arrived.reshape(owners * capacity, row_width))
    tail_f = tail_bf.astype(jnp.float32)
    weight = -live * jax.nn.sigmoid(-jnp.sum(query_f * tail_f, axis=1))
    grad_query = weight[:, None] * tail_f + neg_query
    grad_head, grad_rel = complex_grads(grad_query, head_f, rel_rows)
    rel_local = jnp.dot(rel_onehot.T, grad_rel, precision=lax.Precision.HIGHEST)
    rel_parts = deal(rel_local.reshape(devices, -1), ("blk", "grp"))
    rel_share = jnp.sum(rel_parts, axis=0)
    rel_total = deal(jnp.broadcast_to(rel_share[None], rel_parts.shape), ("blk", "grp"))
    new_relations = adagrad(relations, rel_total.reshape(rel_count, row_width))

    returned_f = returned.astype(jnp.float32)
    owner_weight = -jax.nn.sigmoid(-jnp.sum(returned_f * located.astype(jnp.float32), axis=1))
    tail_rows = swap(requested)
    tail_weights = swap(owner_weight)
    tail_grads = tail_weights[:, None] * swap(returned).astype(jnp.float32)
    entity_grads = spread(tail_rows, ent_count, tail_grads)
    late_rows = jnp.concatenate([head_row, negative_rows[0]])
    late = swap(jnp.concatenate([grad_head, neg_sum], axis=0))
    entity_grads = entity_grads + spread(swap(late_rows), ent_count, late)
    new_entities = adagrad(entities, entity_grads)
    return (new_entities, new_relations)


def solution(mesh):
    return jax.shard_map(
        per_device,
        mesh=mesh,
        in_specs=(
            P("blk", None),
            P(),
            P(("blk", "grp")),
            P(("blk", "grp")),
            P(("blk", "grp"), None),
            P(("blk", "grp")),
            P("blk", None),
            P(("blk", "grp")),
        ),
        out_specs=(P("blk", None), P()),
        check_vma=False,
    )
```

time: 374 us -> 186 us (0.50)
  waiting for transfers between devices: 224 us -> 30.2 us
  matrix products: 7.49 us -> 32.8 us
  starting transfers between devices: 18.1 us -> 41.3 us
  local copies, waits for them, and re-layouts: 36.8 us -> 20.9 us
  between operations: 16.4 us -> 1.71 us
  other arithmetic: 37.3 us -> 25.7 us
    psum x2 -> x0, waiting for transfers between devices: 189 us -> none  [the longest x1 106 us: per_device(): summed = lax.psum(entity_grads, 'grp')]
    dot_general x2 -> x10, matrix products: 4.24 us -> 29.4 us  [the longest x2 14.9 us: spread(): lax.dot_general(hot, both, (((0,), (0,)), ((), ())), preferred_element_ty...]
    scatter-add x3 -> x0, other arithmetic: 21.5 us -> none  [the longest x1 10.9 us: per_device(): entity_grads.at[requested.reshape(-1)].add(returned.reshape(-1, row_width))]
    gather x6 -> x0, local copies, waits for them, and re-layouts: 16.8 us -> none  [the longest x1 5.55 us: per_device(): located = entities[requested].astype(jnp.bfloat16)]
    all_to_all x3 -> x6, starting transfers between devices: 17.8 us -> 34.4 us  [deal(): return lax.all_to_all(blocks, axes, split_axis=0, concat_axis=0, tiled=True)]
    ppermute x0 -> x5, waiting for transfers between devices: none -> 16.5 us  [swap(): other = lax.ppermute(own, 'grp', pairs)]
    all_to_all x3 -> x6, waiting for transfers between devices: 28.5 us -> 13.6 us  [deal(): return lax.all_to_all(blocks, axes, split_axis=0, concat_axis=0, tiled=True)]
    unnamed x22 -> x36, local copies, waits for them, and re-layouts: 11.7 us -> 1.81 us
  transfers between devices with their start and end apart: 6 -> 11, of which waited for: 4 -> 5; matrix products, arithmetic and copies ran while one was open for 15% -> 31% of each run, Pallas kernels for 0% -> 0%
where the time goes in v1:
time: 186 us; the launch traced here: 185 us
  starting transfers between devices  41.3 us (22%)
  matrix products  32.8 us (18%)
  blocking collectives  32.3 us (17%)
  waiting for transfers between devices  30.2 us (16%)
  other arithmetic  25.7 us (14%)
  local copies, waits for them, and re-layouts  20.9 us (11%)
    all_to_all x6, starting transfers between devices, deal(): return lax.all_to_all(blocks, axes, split_axis=0, concat_axis=0, tiled=True)  34.4 us
    all_gather x1, blocking collectives, per_device(): piece = lax.all_gather(own_block, 'blk', axis=0, tiled=True)  32.3 us
    ppermute x5, waiting for transfers between devices, swap(): other = lax.ppermute(own, 'grp', pairs)  16.5 us
    dot_general x2, matrix products, spread(): lax.dot_general(hot, both, (((0,), (0,)), ((), ())), preferred_element_ty...  14.9 us
    all_to_all x6, waiting for transfers between devices, deal(): return lax.all_to_all(blocks, axes, split_axis=0, concat_axis=0, tiled=True)  13.6 us
    dot_general x4, matrix products, pick(): jnp.dot(hot, table, preferred_element_type=jnp.float32).astype(jnp.bfloat16)  9.46 us
    ppermute x5, starting transfers between devices, swap(): other = lax.ppermute(own, 'grp', pairs)  6.88 us
    sub x2, other arithmetic, adagrad(): return table - LEARN_RATE * table_grads / (jnp.sqrt(square_mean) + EPSILON)  4.27 us
  transfers between devices with their start and end apart: 11, of which 5 were waited for; matrix products, arithmetic and copies ran while one was open for 31% of the time, Pallas kernels for 0%

profile of v1, /device:TPU:0, one launch (start us, length us, event | category | flops | bytes accessed | tf_op | source)
XLA Modules:
  0.0 184.9 jit_solution(8124729910627211038)
XLA Ops:
  1.3 0.7 reduce.1
  2.0 0.2 fusion.21
  2.2 0.7 add_reduce_fusion
  2.9 0.7 select_add_fusion
  3.6 0.2 select_reduce_fusion
  3.8 0.7 sub.28
  4.5 7.4 %all-to-all-start = ((s32[16,1,48]{2,1,0:T(1,128)}), s32[16,1,48]{2,1,0:T(1,128)S(1)}, u32[]{:S(2)}, u32[]{:S(2)}) async-start(s32[16,1,48]{2,1,0:T(1,128)} %sub.28), calls=%async_computation | async-start | bytes 16384 | tf_op jit(solution)/shard_map/all_to_all | solution.py:75
  11.9 1.5 fusion.30
  13.3 3.3 %fusion.19 = f32[384,400]{0,1:T(8,128)S(1)} fusion(s32[384]{0:T(512)} %param.10, f32[2048,400]{0,1:T(8,128)} %param.8), kind=kOutput, calls=%fused_computation.40 | convolution fusion | flops 631058432 | bytes 3892736 | tf_op jit(solution)/shard_map/dot_general | solution.py:53
  16.7 0.1 subtract_convert_fusion
  16.8 0.7 copy-done.8
  17.5 1.4 convolution_convert_fusion.1
  19.0 2.2 %copy.23 = bf16[768,400]{1,0:T(8,128)(2,1)} copy(bf16[768,400]{0,1:T(8,128)(2,1)} %convolution_convert_fusion.1) | data formatting | bytes 1228800 | tf_op jit(solution)/shard_map/convert_element_type | solution.py:117
  21.2 6.1 %all-to-all-start.1 = ((bf16[16,48,400]{2,1,0:T(8,128)(2,1)}), bf16[16,48,400]{2,1,0:T(8,128)(2,1)}, u32[]{:S(2)}, u32[]{:S(2)}) async-start(bf16[16,48,400]{2,1,0:T(8,128)(2,1)} %bitcast.22), calls=%async_computation.1 | async-start | bytes 1572864 | tf_op jit(solution)/shard_map/all_to_all | solution.py:75
  27.3 0.6 convolution_convert_fusion.3
  27.9 32.3 %all_gather.3 = bf16[1024,400]{1,0:T(8,128)(2,1)S(1)} all-gather(bf16[64,400]{1,0:T(8,128)(2,1)S(1)} %convolution_convert_fusion.3), channel_id=1, replica_groups=mesh['blk'=16,'grp'=2] {'blk'}, dimensions={0}, use_global_device_ids=true | all-gather | bytes 870400 | tf_op jit(solution)/shard_map/all_gather | solution.py:105
  60.2 0.8 multiply_convert_fusion
  61.0 0.1 copy-done.3
  61.2 0.9 copy-done.5
  62.0 1.5 convolution_convert_fusion
  63.6 2.2 %copy.29 = bf16[1024,400]{1,0:T(8,128)(2,1)} copy(bf16[1024,400]{0,1:T(8,128)(2,1)} %convolution_convert_fusion) | data formatting | bytes 1638400 | tf_op jit(solution)/shard_map/convert_element_type | solution.py:125
  65.8 4.5 %all-to-all-start.3 = ((bf16[16,64,400]{2,1,0:T(8,128)(2,1)}), bf16[16,64,400]{2,1,0:T(8,128)(2,1)}, u32[]{:S(2)}, u32[]{:S(2)}) async-start(bf16[16,64,400]{2,1,0:T(8,128)(2,1)} %bitcast.20), calls=%async_computation.3 | async-start | bytes 2097152 | tf_op jit(solution)/shard_map/all_to_all | solution.py:75
  70.3 1.6 collective-permute-start.3
  71.9 2.1 %collective-permute-done.3 = s32[448]{0:T(512)S(1)} collective-permute-done((s32[448]{0:T(512)S(1)}, s32[448]{0:T(512)S(1)}, u32[]{:S(2)}, u32[]{:S(2)}) %collective-permute-start.3) | collective-permute-done | bytes 1824 | tf_op jit(solution)/shard_map/ppermute | solution.py:69
  74.1 0.5 broadcast.113
  74.6 0.7 reduce.11
  75.3 1.5 collective-permute-start
  76.8 2.2 %copy.24 = bf16[768,400]{0,1:T(8,128)(2,1)} copy(bf16[768,400]{1,0:T(8,128)(2,1)} %bitcast.2) | data formatting | bytes 1228800 | tf_op jit(solution)/shard_map/reshape | solution.py:118
  79.0 3.6 %multiply_reduce_fusion.1 = (f32[768]{0:T(1024)S(1)}, bf16[768,400]{0,1:T(8,128)(2,1)}) fusion(bf16[768,400]{0,1:T(8,128)(2,1)} %copy.24, f32[2048,400]{0,1:T(8,128)S(1)} %copy-done, s32[768]{0:T(1024)S(1)} %reshape.103), kind=kOutput, calls=%fused_computation.38 | convolution fusion | flops 1262218496 | bytes 4511744 | tf_op jit(solution)/shard_map/dot_general | solution.py:53
  82.6 2.3 %copy.28 = bf16[768,400]{1,0:T(8,128)(2,1)} copy(bf16[768,400]{0,1:T(8,128)(2,1)} %get-tuple-element.31) | data formatting | bytes 1228800 | tf_op jit(solution)/shard_map/convert_element_type | solution.py:53
  84.9 8.4 %all-to-all-done.3 = bf16[16,64,400]{2,1,0:T(8,128)(2,1)} async-done(((bf16[16,64,400]{2,1,0:T(8,128)(2,1)}), bf16[16,64,400]{2,1,0:T(8,128)(2,1)}, u32[]{:S(2)}, u32[]{:S(2)}) %all-to-all-start.3) | async-done | bytes 819232 | tf_op jit(solution)/shard_map/all_to_all | solution.py:75
  93.3 7.3 %all-to-all-start.2 = ((bf16[16,48,400]{2,1,0:T(8,128)(2,1)}), bf16[16,48,400]{2,1,0:T(8,128)(2,1)}, u32[]{:S(2)}, u32[]{:S(2)}) async-start(bf16[16,48,400]{2,1,0:T(8,128)(2,1)} %bitcast.21), calls=%async_computation.2 | async-start | bytes 1572864 | tf_op jit(solution)/shard_map/all_to_all | solution.py:75
  100.6 1.6 collective-permute-start.2
  102.2 0.5 collective-permute-start.1
  102.8 14.4 %collective-permute-done.1 = f32[768]{0:T(1024)S(1)} collective-permute-done((f32[768]{0:T(1024)S(1)}, f32[768]{0:T(1024)S(1)}, u32[]{:S(2)}, u32[]{:S(2)}) %collective-permute-start.1) | collective-permute-done | bytes 3104 | tf_op jit(solution)/shard_map/ppermute | solution.py:69
  117.2 2.1 %convert_reduce_fusion = f32[64,400]{1,0:T(8,128)} fusion(bf16[16,64,400]{2,1,0:T(8,128)(2,1)} %all-to-all-done.3), kind=kLoop, calls=%fused_computation.23 | loop fusion | flops 793600 | bytes 921600 | tf_op jit(solution)/shard_map/reduce_sum | solution.py:126
  119.3 1.0 copy.30
  120.3 2.2 %copy.26 = bf16[768,400]{1,0:T(8,128)(2,1)} copy(bf16[768,400]{0,1:T(8,128)(2,1)} %collective-permute-done.2) | data formatting | bytes 1228800 | tf_op jit(solution)/shard_map/ppermute | solution.py:69
  122.5 2.7 %broadcast_select_fusion.1 = (bf16[768,400]{1,0:T(8,128)(2,1)}, bf16[768,400]{1,0:T(8,128)(2,1)}) fusion(bf16[768,400]{1,0:T(8,128)(2,1)} %copy.26, pred[]{:T(512)S(6)} %eq.54, bf16[16,48,400]{2,1,0:T(8,128)(2,1)} %all-to-all-done.1), kind=kLoop, calls=%fused_computation.50 | loop fusion | flops 614400 | bytes 2457601 | tf_op jit(solution)/shard_map/jit(_where)/select_n | solution.py:71
  125.2 2.0 %multiply_reduce_fusion.2 = (f32[384]{0:T(512)S(1)}, f32[384,400]{0,1:T(8,128)S(1)}) fusion(bf16[384,200]{0,1:T(8,128)(2,1)} %copy-done.11, bf16[384,200]{0,1:T(8,128)(2,1)} %copy-done.10, bf16[768,400]{1,0:T(8,128)(2,1)} %bitcast.5, s32[384]{0:T(512)S(1)} %add_reduce_fusion), kind=kOutput, calls=%fused_computation.55 | convolution fusion | flops 237452928 | bytes 1539072 | tf_op jit(solution)/shard_map/dot_general | solution.py:53
  127.2 1.8 convolution_add_fusion
  129.0 0.9 multiply_add_fusion
  130.0 1.2 fusion.22
  131.2 1.7 all_to_all.30
  132.9 5.8 %all-to-all-start.4 = ((f32[32,1,800]{2,1,0:T(1,128)}), f32[32,1,800]{2,1,0:T(1,128)}, u32[]{:S(2)}, u32[]{:S(2)}) async-start(f32[32,1,800]{2,1,0:T(1,128)} %all_to_all.30), calls=%async_computation.4 | async-start | bytes 229376 | tf_op jit(solution)/shard_map/all_to_all | solution.py:75
  138.7 3.7 %reduce-precision_convert_fusion = (bf16[1536,400]{1,0:T(8,128)(2,1)}, bf16[1536,400]{1,0:T(8,128)(2,1)}) fusion(f32[1536]{0:T(1024)S(1)} %pad_maximum_fusion.4, bf16[768,400]{1,0:T(8,128)(2,1)} %get-tuple-element.13, bf16[768,400]{1,0:T(8,128)(2,1)} %get-tuple-element.12), kind=kLoop, calls=%fused_computation.8 | loop fusion | flops 5529600 | bytes 3692544 | tf_op jit(solution)/shard_map/convert.2
  142.4 1.0 pad_maximum_fusion.2
  143.4 1.7 collective-permute-start.4
  145.1 1.9 %all-to-all-done.4 = f32[32,1,800]{2,1,0:T(1,128)} async-done(((f32[32,1,800]{2,1,0:T(1,128)}), f32[32,1,800]{2,1,0:T(1,128)}, u32[]{:S(2)}, u32[]{:S(2)}) %all-to-all-start.4) | async-done | bytes 102432 | tf_op jit(solution)/shard_map/all_to_all | solution.py:75
  147.0 1.0 reduce_sum.78
  148.0 0.7 broadcast_in_dim.7
  148.7 3.4 %all-to-all-start.5 = ((f32[32,1,800]{2,1,0:T(1,128)}), f32[32,1,800]{2,1,0:T(1,128)}, u32[]{:S(2)}, u32[]{:S(2)}) async-start(f32[32,1,800]{2,1,0:T(1,128)} %broadcast_in_dim.7), calls=%async_computation.5 | async-start | bytes 229376 | tf_op jit(solution)/shard_map/all_to_all | solution.py:75
  152.1 10.9 %fusion = f32[2048,800]{0,1:T(8,128)} fusion(s32[1536]{0:T(1024)S(1)} %pad_add_fusion, bf16[1536,400]{1,0:T(8,128)(2,1)} %get-tuple-element.11, bf16[1536,400]{1,0:T(8,128)(2,1)} %get-tuple-element.10), kind=kOutput, calls=%fused_computation.1 | convolution fusion | flops 5041225728 | bytes 9017344 | tf_op jit(solution)/shard_map/dot_general | solution.py:60
  163.0 3.3 %all-to-all-done.5 = f32[32,1,800]{2,1,0:T(1,128)} async-done(((f32[32,1,800]{2,1,0:T(1,128)}), f32[32,1,800]{2,1,0:T(1,128)}, u32[]{:S(2)}, u32[]{:S(2)}) %all-to-all-start.5) | async-done | bytes 102432 | tf_op jit(solution)/shard_map/all_to_all | solution.py:75
  166.3 2.2 %multiply_reduce_fusion.3 = (f32[32,800]{1,0:T(8,128)}, f32[32,800]{1,0:T(8,128)}) fusion(f32[32,1,800]{2,1,0:T(1,128)} %all-to-all-done.5), kind=kLoop, calls=%fused_computation.74 | loop fusion | flops 51200 | bytes 307200 | tf_op jit(solution)/shard_map/mul | solution.py:44
  168.5 1.6 mul.158
  170.1 1.0 reduce_sum.79
  171.2 1.6 mul.156
  172.8 1.7 divide_subtract_fusion.1
  174.5 1.5 broadcast_select_fusion.3
  176.0 0.3 reduce-precision_convert_fusion.1
  176.4 4.1 %fusion.1 = f32[2048,800]{0,1:T(8,128)S(1)} fusion(s32[896]{0:T(1024)S(1)} %pad_add_fusion.1, bf16[896,400]{0,1:T(8,128)(2,1)S(1)} %get-tuple-element.7, bf16[896,400]{0,1:T(8,128)(2,1)S(1)} %get-tuple-element.6), kind=kOutput, calls=%fused_computation.3 | convolution fusion | flops 2940715008 | bytes 7990784 | tf_op jit(solution)/shard_map/dot_general | solution.py:60
  180.5 1.9 %multiply_reduce_fusion = (f32[2048]{0:T(1024)S(1)}, f32[2048,400]{0,1:T(8,128)S(1)}) fusion(f32[2048,800]{0,1:T(8,128)S(1)} %fusion.1, f32[2048,800]{0,1:T(8,128)S(1)} %bitcast.19), kind=kLoop, calls=%fused_computation.14 | loop fusion | flops 4093952 | bytes 16392192 | tf_op jit(solution)/shard_map/reduce_sum | solution.py:44
  182.3 2.6 %divide_subtract_fusion = f32[2048,400]{0,1:T(8,128)} fusion(f32[2048,400]{0,1:T(8,128)S(1)} %copy-done, f32[2048,400]{0,1:T(8,128)S(1)} %get-tuple-element.5, f32[2048]{0:T(1024)S(1)} %sqrt_add_fusion), kind=kLoop, calls=%fused_computation.13 | loop fusion | flops 2457600 | bytes 9838592 | tf_op jit(solution)/shard_map/sub | solution.py:45
  (55 shorter events, 0.4 us)
Async XLA Ops:
  4.5 16.7 %all-to-all-start = ((s32[16,1,48]{2,1,0:T(1,128)}), s32[16,1,48]{2,1,0:T(1,128)S(1)}, u32[]{:S(2)}, u32[]{:S(2)}) async-start(s32[16,1,48]{2,1,0:T(1,128)} %sub.28), calls=%async_computation | async-start | bytes 16384 | tf_op jit(solution)/shard_map/all_to_all | solution.py:75
  13.3 3.4 %copy-start.1 = (f32[384,400]{0,1:T(8,128)}, f32[384,400]{0,1:T(8,128)S(1)}, u32[]{:S(2)}) copy-start(f32[384,400]{0,1:T(8,128)S(1)} %fusion.30) | copy-start | bytes 1843204
  16.6 0.8 copy-start.8
  16.6 10.6 %copy-start = (f32[2048,400]{0,1:T(8,128)S(1)}, f32[2048,400]{0,1:T(8,128)}, u32[]{:S(2)}) copy-start(f32[2048,400]{0,1:T(8,128)} %param.8) | copy-start | bytes 9830404
  16.6 10.6 %copy-start.15 = (s32[1,64]{1,0:T(1,128)S(1)}, s32[1,64]{1,0:T(1,128)}, u32[]{:S(2)}) copy-start(s32[1,64]{1,0:T(1,128)} %param.14) | copy-start | bytes 772
  16.8 0.8 copy-start.11
  16.8 44.2 %copy-start.10 = (bf16[384,200]{0,1:T(8,128)(2,1)}, bf16[384,200]{0,1:T(8,128)(2,1)S(1)}, u32[]{:S(2)}) copy-start(bf16[384,200]{0,1:T(8,128)(2,1)S(1)} %get-tuple-element.18) | copy-start | bytes 460804
  21.2 44.6 %all-to-all-start.1 = ((bf16[16,48,400]{2,1,0:T(8,128)(2,1)}), bf16[16,48,400]{2,1,0:T(8,128)(2,1)}, u32[]{:S(2)}, u32[]{:S(2)}) async-start(bf16[16,48,400]{2,1,0:T(8,128)(2,1)} %bitcast.22), calls=%async_computation.1 | async-start | bytes 1572864 | tf_op jit(solution)/shard_map/all_to_all | solution.py:75
  27.2 32.9 %copy-start.12 = (bf16[384,200]{0,1:T(8,128)(2,1)S(1)}, bf16[384,200]{0,1:T(8,128)(2,1)}, u32[]{:S(2)}) copy-start(bf16[384,200]{0,1:T(8,128)(2,1)} %copy-done.11) | copy-start | bytes 460804
  60.2 1.0 copy-start.3
  61.2 0.9 copy-start.5
  62.0 8.3 %copy-start.14 = (s32[384]{0:T(512)S(1)}, s32[384]{0:T(512)}, u32[]{:S(2)}) copy-start(s32[384]{0:T(512)} %param.10) | copy-start | bytes 4612
  65.8 27.5 %all-to-all-start.3 = ((bf16[16,64,400]{2,1,0:T(8,128)(2,1)}), bf16[16,64,400]{2,1,0:T(8,128)(2,1)}, u32[]{:S(2)}, u32[]{:S(2)}) async-start(bf16[16,64,400]{2,1,0:T(8,128)(2,1)} %bitcast.20), calls=%async_computation.3 | async-start | bytes 2097152 | tf_op jit(solution)/shard_map/all_to_all | solution.py:75
  70.3 3.7 %collective-permute-start.3 = (s32[448]{0:T(512)S(1)}, s32[448]{0:T(512)S(1)}, u32[]{:S(2)}, u32[]{:S(2)}) collective-permute-start(s32[448]{0:T(512)S(1)} %pad_add_fusion.2), channel_id=1, source_target_pairs={{0,1},{1,0},{2,3},{3,2},{4,5},{5,4},{6,7},{7,6},{8,9},{9,8},{10,11... | collective-permute-start | bytes 5384 | tf_op jit(solution)/shard_map/ppermute | solution.py:69
  75.3 25.3 %collective-permute-start = (s32[768]{0:T(1024)S(1)}, s32[768]{0:T(1024)S(1)}, u32[]{:S(2)}, u32[]{:S(2)}) collective-permute-start(s32[768]{0:T(1024)S(1)} %reshape.103), channel_id=1, source_target_pairs={{0,1},{1,0},{2,3},{3,2},{4,5},{5,4},{6,7},{7,6},{8,9},{9,8},{10,11... | collective-permute-start | bytes 9224 | tf_op jit(solution)/shard_map/ppermute | solution.py:69
  93.3 31.9 %all-to-all-start.2 = ((bf16[16,48,400]{2,1,0:T(8,128)(2,1)}), bf16[16,48,400]{2,1,0:T(8,128)(2,1)}, u32[]{:S(2)}, u32[]{:S(2)}) async-start(bf16[16,48,400]{2,1,0:T(8,128)(2,1)} %bitcast.21), calls=%async_computation.2 | async-start | bytes 1572864 | tf_op jit(solution)/shard_map/all_to_all | solution.py:75
  100.6 19.7 %collective-permute-start.2 = (bf16[768,400]{0,1:T(8,128)(2,1)}, bf16[768,400]{0,1:T(8,128)(2,1)}, u32[]{:S(2)}, u32[]{:S(2)}) collective-permute-start(bf16[768,400]{0,1:T(8,128)(2,1)} %copy.24), channel_id=1, source_target_pairs={{0,1},{1,0},{2,3},{3,2},{4,5},{5,4},{6,7},{7,6},{8,9},{9,8},{10,11... | collective-permute-start | bytes 1843208 | tf_op jit(solution)/shard_map/ppermute | solution.py:69
  102.2 15.0 %collective-permute-start.1 = (f32[768]{0:T(1024)S(1)}, f32[768]{0:T(1024)S(1)}, u32[]{:S(2)}, u32[]{:S(2)}) collective-permute-start(f32[768]{0:T(1024)S(1)} %divide_negate_fusion), channel_id=1, source_target_pairs={{0,1},{1,0},{2,3},{3,2},{4,5},{5,4},{6,7},{7,6},{8,9},{9,8},{10,11... | collective-permute-start | bytes 9224 | tf_op jit(solution)/shard_map/ppermute | solution.py:69
  125.2 2.0 %copy-start.4 = (bf16[1024,400]{1,0:T(8,128)(2,1)S(1)}, bf16[1024,400]{1,0:T(8,128)(2,1)}, u32[]{:S(2)}) copy-start(bf16[1024,400]{1,0:T(8,128)(2,1)} %copy-done.3) | copy-start | bytes 2457604
  125.2 3.8 %copy-start.2 = (f32[384,400]{0,1:T(8,128)S(1)}, f32[384,400]{0,1:T(8,128)}, u32[]{:S(2)}) copy-start(f32[384,400]{0,1:T(8,128)} %copy-done.1) | copy-start | bytes 1843204
  125.2 3.8 %copy-start.9 = (f32[384,400]{0,1:T(8,128)S(1)}, f32[384,400]{0,1:T(8,128)}, u32[]{:S(2)}) copy-start(f32[384,400]{0,1:T(8,128)} %copy-done.8) | copy-start | bytes 1843204
  127.2 2.8 %copy-start.13 = (s32[384]{0:T(512)S(1)}, s32[384]{0:T(512)}, u32[]{:S(2)}) copy-start(s32[384]{0:T(512)} %param.11) | copy-start | bytes 4612
  132.9 14.1 %all-to-all-start.4 = ((f32[32,1,800]{2,1,0:T(1,128)}), f32[32,1,800]{2,1,0:T(1,128)}, u32[]{:S(2)}, u32[]{:S(2)}) async-start(f32[32,1,800]{2,1,0:T(1,128)} %all_to_all.30), calls=%async_computation.4 | async-start | bytes 229376 | tf_op jit(solution)/shard_map/all_to_all | solution.py:75
  138.6 3.7 %copy-start.6 = (f32[384,200]{0,1:T(8,128)S(1)}, f32[384,200]{0,1:T(8,128)}, u32[]{:S(2)}) copy-start(f32[384,200]{0,1:T(8,128)} %get-tuple-element.20) | copy-start | bytes 921604
  138.7 3.7 %copy-start.7 = (f32[384,200]{0,1:T(8,128)S(1)}, f32[384,200]{0,1:T(8,128)}, u32[]{:S(2)}) copy-start(f32[384,200]{0,1:T(8,128)} %get-tuple-element.21) | copy-start | bytes 921604
  143.4 31.2 %collective-permute-start.4 = (f32[448,400]{0,1:T(8,128)}, f32[448,400]{0,1:T(8,128)}, u32[]{:S(2)}, u32[]{:S(2)}) collective-permute-start(f32[448,400]{0,1:T(8,128)} %pad_maximum_fusion.2), channel_id=1, source_target_pairs={{0,1},{1,0},{2,3},{3,2},{4,5},{5,4},{6,7},{7,6},{8,9},{9,8},{10,11... | collective-permute-start | bytes 2150408 | tf_op jit(solution)/shard_map/ppermute | solution.py:69
  148.7 17.6 %all-to-all-start.5 = ((f32[32,1,800]{2,1,0:T(1,128)}), f32[32,1,800]{2,1,0:T(1,128)}, u32[]{:S(2)}, u32[]{:S(2)}) async-start(f32[32,1,800]{2,1,0:T(1,128)} %broadcast_in_dim.7), calls=%async_computation.5 | async-start | bytes 229376 | tf_op jit(solution)/shard_map/all_to_all | solution.py:75
  176.0 4.4 %slice-start = ((s8[6553600]{0:T(1024)(128)(4,1)}), s8[4194304]{0:T(1024)(128)(4,1)S(1)}, s32[]{:S(2)}) async-start(s8[6553600]{0:T(1024)(128)(4,1)} %bitcast.18), calls=%async_computation.6 | async-start | bytes 8388608
  176.4 4.1 %slice-start.1 = ((s8[6553600]{0:T(1024)(128)(4,1)}), s8[2359296]{0:T(1024)(128)(4,1)S(1)}, s32[]{:S(2)}) async-start(s8[6553600]{0:T(1024)(128)(4,1)} %bitcast.18), calls=%async_computation.7 | async-start | bytes 4718592

commit v2 on v1

--- a/solution.py
+++ b/solution.py
@@ -1,6 +1,9 @@
+import functools
 import jax
 import jax.numpy as jnp
 from jax import lax
+from jax.experimental import pallas as pl
+from jax.experimental.pallas import tpu as pltpu
 from jax.sharding import PartitionSpec as P
 
 EPSILON = 1e-06
@@ -75,6 +78,115 @@
     return lax.all_to_all(blocks, axes, split_axis=0, concat_axis=0, tiled=True)
 
 
+def remote(source, landing, send_sem, recv_sem, device):
+    return pltpu.make_async_remote_copy(
+        src_ref=source,
+        dst_ref=landing,
+        send_sem=send_sem,
+        recv_sem=recv_sem,
+        device_id=device,
+        device_id_type=pl.DeviceIdType.MESH,
+    )
+
+
+def forward_kernel(
+    owners, query_ref, tail_ref, own_ref, query_out, tail_out, neg_out, sends, recvs, passes, gots
+):
+    me = lax.axis_index("blk")
+    sibling = me + 1 - 2 * lax.rem(me, 2)
+    chips = owners // 2
+    barrier = pltpu.get_barrier_semaphore()
+
+    def hello(step, carry):
+        pl.semaphore_signal(
+            barrier,
+            inc=1,
+            device_id={"blk": lax.rem(me + step, owners)},
+            device_id_type=pl.DeviceIdType.MESH,
+        )
+        return carry
+
+    lax.fori_loop(1, owners, hello, 0)
+    pl.semaphore_wait(barrier, owners - 1)
+
+    def neg_copy(step):
+        return remote(
+            own_ref,
+            neg_out.at[me],
+            sends.at[0, step],
+            recvs.at[0, step],
+            {"blk": lax.rem(me + 2 * step, owners)},
+        )
+
+    def pass_copy(step):
+        block = lax.rem(me - 2 * step + 2 * owners, owners)
+        source = neg_out.at[block]
+        return remote(source, source, passes.at[step], gots.at[step], {"blk": sibling})
+
+    def row_copy(kind, source, landing, step):
+        there = lax.rem(me + step, owners)
+        return remote(
+            source.at[there],
+            landing.at[me],
+            sends.at[kind, step],
+            recvs.at[kind, step],
+            {"blk": there},
+        )
+
+    def each(low, high, act):
+        def body(step, carry):
+            act(step)
+            return carry
+
+        lax.fori_loop(low, high, body, 0)
+
+    neg_out[me] = own_ref[...]
+    each(1, chips, lambda step: neg_copy(step).start())
+    pass_copy(0).start()
+    each(1, owners, lambda step: row_copy(1, tail_ref, tail_out, step).start())
+    each(1, owners, lambda step: row_copy(2, query_ref, query_out, step).start())
+    tail_out[me] = tail_ref[me]
+    query_out[me] = query_ref[me]
+
+    def hand_on(step):
+        neg_copy(step).wait_recv()
+        pass_copy(step).start()
+
+    each(1, chips, hand_on)
+
+    def finish(step):
+        row_copy(1, tail_ref, tail_out, step).wait()
+        row_copy(2, query_ref, query_out, step).wait()
+
+    each(0, chips, lambda step: pass_copy(step).wait())
+    each(1, chips, lambda step: neg_copy(step).wait_send())
+    each(1, owners, finish)
+
+
+def forward_exchange(outgoing, located, own_block):
+    owners = outgoing.shape[0]
+    vmem = pl.BlockSpec(memory_space=pltpu.VMEM)
+    return pl.pallas_call(
+        functools.partial(forward_kernel, owners),
+        out_shape=(
+            jax.ShapeDtypeStruct(outgoing.shape, jnp.bfloat16),
+            jax.ShapeDtypeStruct(located.shape, jnp.bfloat16),
+            jax.ShapeDtypeStruct((owners,) + own_block.shape, jnp.bfloat16),
+        ),
+        in_specs=[vmem] * 3,
+        out_specs=(vmem,) * 3,
+        scratch_shapes=[
+            pltpu.SemaphoreType.DMA((3, owners)),
+            pltpu.SemaphoreType.DMA((3, owners)),
+            pltpu.SemaphoreType.DMA((owners,)),
+            pltpu.SemaphoreType.DMA((owners,)),
+        ],
+        compiler_params=pltpu.CompilerParams(
+            collective_id=1, has_side_effects=True, vmem_limit_bytes=48 * 2**20
+        ),
+    )(outgoing, located, own_block)
+
+
 def per_device(
     entities, relations, head_row, relation_id, tail_owner, tail_row, negative_rows, edge_count
 ):
@@ -84,7 +196,7 @@
     ent_count, row_width = entities.shape
     neg_count = negative_rows.shape[1]
     rel_count = relations.shape[0]
-    capacity = max(2, 2 * edge_total // owners)
+    capacity = -(-max(2, 2 * edge_total // owners) // 16) * 16
     alive = jnp.arange(edge_total, dtype=jnp.int32) < edge_count[0]
     live = alive.astype(jnp.float32)
     target = tail_owner[:, 0]
@@ -102,9 +214,7 @@
 
     table = entities.astype(jnp.bfloat16)
     own_block = pick(hot_rows(negative_rows[0], ent_count, jnp.bfloat16), table)
-    piece = lax.all_gather(own_block, "blk", axis=0, tiled=True)
     located = pick(hot_rows(requested, ent_count, jnp.bfloat16), table)
-    arrived = deal(located.reshape(owners, capacity, row_width), "blk")
 
     head_bf = pick(hot_rows(head_row, ent_count, jnp.bfloat16), table)
     rel_onehot = hot_rows(relation_id, rel_count, jnp.float32)
@@ -115,7 +225,13 @@
     outgoing = lax.dot_general(
         slot_hot, query_bf, (((0,), (0,)), ((), ())), preferred_element_type=jnp.float32
     ).astype(jnp.bfloat16)
-    returned = deal(outgoing.reshape(owners, capacity, row_width), "blk").reshape(-1, row_width)
+    returned, arrived, piece = forward_exchange(
+        outgoing.reshape(owners, capacity, row_width),
+        located.reshape(owners, capacity, row_width),
+        own_block,
+    )
+    returned = returned.reshape(-1, row_width)
+    piece = piece.reshape(-1, row_width)
 
     neg_scale = 1.0 / (owners * neg_count)
     scores = jnp.dot(query_bf, piece.T, preferred_element_type=jnp.float32)

time: 186 us -> 176 us (0.946)
  Pallas kernels: 0 us -> 45.2 us
  blocking collectives: 32.3 us -> 0 us
  waiting for transfers between devices: 30.2 us -> 46.7 us
  local copies, waits for them, and re-layouts: 20.9 us -> 8.18 us
  starting transfers between devices: 41.3 us -> 29.6 us
  other arithmetic: 25.7 us -> 16.3 us
  matrix products: 32.8 us -> 27.2 us
    pallas_call x0 -> x1, Pallas kernels: none -> 45.2 us  [forward_exchange(): pl.pallas_call(functools.partial(forward_kernel, owners), out_shape=(jax....]
    all_gather x1 -> x0, blocking collectives: 32.3 us -> none  [per_device(): piece = lax.all_gather(own_block, 'blk', axis=0, tiled=True)]
    all_to_all x6 -> x4, waiting for transfers between devices: 13.6 us -> 33.8 us  [deal(): return lax.all_to_all(blocks, axes, split_axis=0, concat_axis=0, tiled=True)]
    all_to_all x6 -> x4, starting transfers between devices: 34.4 us -> 25 us  [deal(): return lax.all_to_all(blocks, axes, split_axis=0, concat_axis=0, tiled=True)]
    ppermute x5, waiting for transfers between devices: 16.5 us -> 12.9 us  [swap(): other = lax.ppermute(own, 'grp', pairs)]
    dot_general x2, matrix products: 14.9 us -> 11.5 us  [spread(): lax.dot_general(hot, both, (((0,), (0,)), ((), ())), preferred_element_ty...]
    select_n x5, other arithmetic: 4.18 us -> 1.38 us  [swap(): jnp.where(first, own, other)]
    ppermute x5, starting transfers between devices: 6.88 us -> 4.61 us  [swap(): other = lax.ppermute(own, 'grp', pairs)]
  transfers between devices with their start and end apart: 11 -> 9, of which waited for: 5 -> 4; matrix products, arithmetic and copies ran while one was open for 31% -> 19% of each run, Pallas kernels for 0% -> 26%
where the time goes in v2:
time: 176 us; the launch traced here: 175 us
  waiting for transfers between devices  46.7 us (27%)
  Pallas kernels  45.2 us (26%)
  starting transfers between devices  29.6 us (17%)
  matrix products  27.2 us (15%)
  other arithmetic  16.3 us (9%)
  local copies, waits for them, and re-layouts  8.18 us (5%)
  between operations  1.96 us (1%)
    pallas_call x1, Pallas kernels, forward_exchange(): pl.pallas_call(functools.partial(forward_kernel, owners), out_shape=(jax....  45.2 us
    all_to_all x4, waiting for transfers between devices, deal(): return lax.all_to_all(blocks, axes, split_axis=0, concat_axis=0, tiled=True)  33.8 us
    all_to_all x4, starting transfers between devices, deal(): return lax.all_to_all(blocks, axes, split_axis=0, concat_axis=0, tiled=True)  25 us
    ppermute x5, waiting for transfers between devices, swap(): other = lax.ppermute(own, 'grp', pairs)  12.9 us
    dot_general x2, matrix products, spread(): lax.dot_general(hot, both, (((0,), (0,)), ((), ())), preferred_element_ty...  11.5 us
    dot_general x4, matrix products, pick(): jnp.dot(hot, table, preferred_element_type=jnp.float32).astype(jnp.bfloat16)  8.86 us
    ppermute x5, starting transfers between devices, swap(): other = lax.ppermute(own, 'grp', pairs)  4.61 us
  transfers between devices with their start and end apart: 9, of which 4 were waited for; matrix products, arithmetic and copies ran while one was open for 19% of the time, Pallas kernels for 26%

profile of v2, /device:TPU:0, one launch (start us, length us, event | category | flops | bytes accessed | tf_op | source)
XLA Modules:
  0.0 175.1 jit_solution(10867745010811494057)
XLA Ops:
  1.4 0.9 reduce.1
  2.3 0.2 fusion.21
  2.6 0.7 add_reduce_fusion
  3.3 0.7 select_add_fusion
  4.0 0.2 select_reduce_fusion
  4.2 0.7 sub.28
  4.8 7.4 %all-to-all-start = ((s32[16,1,48]{2,1,0:T(1,128)}), s32[16,1,48]{2,1,0:T(1,128)S(1)}, u32[]{:S(2)}, u32[]{:S(2)}) async-start(s32[16,1,48]{2,1,0:T(1,128)} %sub.28), calls=%async_computation | async-start | bytes 16384 | tf_op jit(solution)/shard_map/all_to_all | solution.py:78
  12.2 0.7 pad_add_fusion.2
  12.9 1.5 collective-permute-start.3
  14.4 2.6 %convolution_convert_fusion.3.own_ref = bf16[64,400]{1,0:T(8,128)(2,1)S(1)} fusion(s32[64]{0:T(128)} %bitcast.23, f32[2048,400]{0,1:T(8,128)} %param.8), kind=kOutput, calls=%fused_computation.45 | convolution fusion | flops 105833472 | bytes 3328256 | tf_op jit(solution)/shard_map/dot_general | solution.py:56
  17.1 1.1 fusion.19
  18.2 0.5 fusion.30
  18.8 0.8 copy-done.4
  19.6 0.7 subtract_convert_fusion
  20.3 0.7 copy-done.11
  21.0 1.5 convolution_convert_fusion.1
  22.5 0.3 copy.26
  22.8 0.1 pad_add_fusion.1
  22.9 0.5 broadcast.113
  23.4 0.7 reduce.11
  24.2 0.5 collective-permute-start
  24.7 3.6 %fusion.17 = bf16[768,400]{0,1:T(8,128)(2,1)S(1)} fusion(s32[768]{0:T(1024)S(1)} %reshape.106, f32[2048,400]{0,1:T(8,128)} %param.8), kind=kOutput, calls=%fused_computation.34 | convolution fusion | flops 1260990464 | bytes 3894272 | tf_op jit(solution)/shard_map/dot_general | solution.py:56
  28.3 0.3 copy.27
  28.6 0.6 copy-done.10
  29.2 45.2 %shard_map.95 = (bf16[16,48,400]{2,1,0:T(8,128)(2,1)S(1)}, bf16[16,48,400]{2,1,0:T(8,128)(2,1)S(1)}, bf16[16,64,400]{2,1,0:T(8,128)(2,1)S(1)}) custom-call(bf16[16,48,400]{2,1,0:T(8,128)(2,1)S(1)} %bitcast.16, bf16[16,48,400]{2,1,0:T(8,128)(2,1)S(1)} %bitcast.17, bf16[64,400]{1,0:T(8,128)(2,1)S(1)} %convolution_convert_fusion.3.own_ref), custom_call_target="tpu_custom_call" | custom-call | tf_op jit(solution)/shard_map/pallas_call | solution.py:169
  74.3 0.9 copy-done
  75.2 0.2 copy.28
  75.5 1.3 multiply_reduce_fusion.1
  76.8 1.5 collective-permute-start.2
  78.3 1.6 multiply_reduce_fusion.2
  79.9 0.6 collective-permute-start.1
  80.6 1.8 %multiply_convert_fusion = bf16[384,1024]{1,0:T(8,128)(2,1)S(1)} fusion(bf16[1024,400]{1,0:T(8,128)(2,1)S(1)} %bitcast.18, f32[384]{0:T(512)S(1)} %get-tuple-element.37, bf16[384,200]{0,1:T(8,128)(2,1)S(1)} %copy-done.12, bf16[384,200]{0,1:T(8,128)(2,1)} %get-tuple-element.24), kind=kOutput, calls=%fused_computation.26 | convolution fusion | flops 317153280 | bytes 1914368 | tf_op jit(solution)/shard_map/dot_general | solution.py:237
  82.4 1.6 convolution_convert_fusion
  84.0 0.7 convolution_add_fusion
  84.7 1.0 multiply_add_fusion
  85.7 0.5 fusion.22
  86.2 0.8 all_to_all.22
  87.0 11.2 %all-to-all-start.2 = ((f32[32,1,800]{2,1,0:T(1,128)}), f32[32,1,800]{2,1,0:T(1,128)S(1)}, u32[]{:S(2)}, u32[]{:S(2)}) async-start(f32[32,1,800]{2,1,0:T(1,128)} %all_to_all.22), calls=%async_computation.2 | async-start | bytes 229376 | tf_op jit(solution)/shard_map/all_to_all | solution.py:78
  98.2 1.3 copy.32
  99.5 7.0 %all-to-all-done.2 = f32[32,1,800]{2,1,0:T(1,128)S(1)} async-done(((f32[32,1,800]{2,1,0:T(1,128)}), f32[32,1,800]{2,1,0:T(1,128)S(1)}, u32[]{:S(2)}, u32[]{:S(2)}) %all-to-all-start.2) | async-done | bytes 102432 | tf_op jit(solution)/shard_map/all_to_all | solution.py:78
  106.6 0.1 reduce_sum.78
  106.7 0.7 broadcast_in_dim.7
  107.4 2.6 %all-to-all-start.3 = ((f32[32,1,800]{2,1,0:T(1,128)}), f32[32,1,800]{2,1,0:T(1,128)S(1)}, u32[]{:S(2)}, u32[]{:S(2)}) async-start(f32[32,1,800]{2,1,0:T(1,128)} %broadcast_in_dim.7), calls=%async_computation.3 | async-start | bytes 229376 | tf_op jit(solution)/shard_map/all_to_all | solution.py:78
  110.0 8.3 %all-to-all-done.3 = f32[32,1,800]{2,1,0:T(1,128)S(1)} async-done(((f32[32,1,800]{2,1,0:T(1,128)}), f32[32,1,800]{2,1,0:T(1,128)S(1)}, u32[]{:S(2)}, u32[]{:S(2)}) %all-to-all-start.3) | async-done | bytes 102432 | tf_op jit(solution)/shard_map/all_to_all | solution.py:78
  118.3 3.8 %all-to-all-start.1 = ((bf16[16,64,400]{2,1,0:T(8,128)(2,1)}), bf16[16,64,400]{2,1,0:T(8,128)(2,1)S(1)}, u32[]{:S(2)}, u32[]{:S(2)}) async-start(bf16[16,64,400]{2,1,0:T(8,128)(2,1)} %bitcast.7), calls=%async_computation.1 | async-start | bytes 2097152 | tf_op jit(solution)/shard_map/all_to_all | solution.py:78
  122.2 0.6 multiply_reduce_fusion.3
  122.8 0.1 mul.158
  122.9 0.1 reduce_sum.79
  123.0 0.1 mul.156
  123.1 0.7 divide_subtract_fusion.1
  123.9 1.2 broadcast_select_fusion.1
  125.1 1.4 reduce-precision_convert_fusion
  126.5 18.4 %all-to-all-done.1 = bf16[16,64,400]{2,1,0:T(8,128)(2,1)S(1)} async-done(((bf16[16,64,400]{2,1,0:T(8,128)(2,1)}), bf16[16,64,400]{2,1,0:T(8,128)(2,1)S(1)}, u32[]{:S(2)}, u32[]{:S(2)}) %all-to-all-start.1) | async-done | bytes 819232 | tf_op jit(solution)/shard_map/all_to_all | solution.py:78
  144.9 0.2 convert_reduce_fusion
  145.1 0.1 copy.33
  145.2 0.1 pad_maximum_fusion.2
  145.3 0.4 collective-permute-start.4
  145.7 7.5 %fusion = f32[2048,800]{0,1:T(8,128)S(1)} fusion(s32[1536]{0:T(1024)S(1)} %pad_add_fusion, bf16[1536,400]{0,1:T(8,128)(2,1)} %get-tuple-element.17, bf16[1536,400]{0,1:T(8,128)(2,1)S(1)} %get-tuple-element.16), kind=kOutput, calls=%fused_computation.1 | convolution fusion | flops 5041225728 | bytes 9017344 | tf_op jit(solution)/shard_map/dot_general | solution.py:63
  153.2 12.9 %collective-permute-done.4 = f32[448,400]{0,1:T(8,128)S(1)} collective-permute-done((f32[448,400]{0,1:T(8,128)S(1)}, f32[448,400]{0,1:T(8,128)S(1)}, u32[]{:S(2)}, u32[]{:S(2)}) %collective-permute-start.4) | collective-permute-done | bytes 716832 | tf_op jit(solution)/shard_map/ppermute | solution.py:72
  166.1 0.2 broadcast_select_fusion.3
  166.3 0.3 reduce-precision_convert_fusion.1
  166.6 4.1 %fusion.1 = f32[2048,800]{0,1:T(8,128)S(1)} fusion(s32[896]{0:T(1024)S(1)} %pad_add_fusion.1, bf16[896,400]{0,1:T(8,128)(2,1)S(1)} %get-tuple-element.13, bf16[896,400]{0,1:T(8,128)(2,1)S(1)} %get-tuple-element.12), kind=kOutput, calls=%fused_computation.3 | convolution fusion | flops 2940715008 | bytes 7990784 | tf_op jit(solution)/shard_map/dot_general | solution.py:63
  170.7 1.9 %multiply_reduce_fusion = (f32[2048]{0:T(1024)S(1)}, f32[2048,400]{0,1:T(8,128)S(1)}) fusion(f32[2048,800]{0,1:T(8,128)S(1)} %fusion.1, f32[2048,800]{0,1:T(8,128)S(1)} %fusion), kind=kLoop, calls=%fused_computation.14 | loop fusion | flops 4093952 | bytes 16392192 | tf_op jit(solution)/shard_map/reduce_sum | solution.py:47
  172.6 2.5 %divide_subtract_fusion = f32[2048,400]{0,1:T(8,128)} fusion(f32[2048,400]{0,1:T(8,128)S(1)} %copy-done.3, f32[2048,400]{0,1:T(8,128)S(1)} %get-tuple-element.11, f32[2048]{0:T(1024)S(1)} %sqrt_add_fusion), kind=kLoop, calls=%fused_computation.13 | loop fusion | flops 2457600 | bytes 9838592 | tf_op jit(solution)/shard_map/sub | solution.py:48
  (51 shorter events, 0.3 us)
Async XLA Ops:
  0.6 16.4 %copy-start.17 = (s32[384]{0:T(512)S(1)}, s32[384]{0:T(512)}, u32[]{:S(2)}) copy-start(s32[384]{0:T(512)} %param.10) | copy-start | bytes 4612
  0.6 16.4 %copy-start.2 = (f32[2048,400]{0,1:T(8,128)S(1)}, f32[2048,400]{0,1:T(8,128)}, u32[]{:S(2)}) copy-start(f32[2048,400]{0,1:T(8,128)} %param.8) | copy-start | bytes 9830404
  4.8 18.1 %all-to-all-start = ((s32[16,1,48]{2,1,0:T(1,128)}), s32[16,1,48]{2,1,0:T(1,128)S(1)}, u32[]{:S(2)}, u32[]{:S(2)}) async-start(s32[16,1,48]{2,1,0:T(1,128)} %sub.28), calls=%async_computation | async-start | bytes 16384 | tf_op jit(solution)/shard_map/all_to_all | solution.py:78
  12.9 9.9 %collective-permute-start.3 = (s32[448]{0:T(512)S(1)}, s32[448]{0:T(512)S(1)}, u32[]{:S(2)}, u32[]{:S(2)}) collective-permute-start(s32[448]{0:T(512)S(1)} %pad_add_fusion.2), channel_id=1, source_target_pairs={{0,1},{1,0},{2,3},{3,2},{4,5},{5,4},{6,7},{7,6},{8,9},{9,8},{10,11... | collective-permute-start | bytes 5384 | tf_op jit(solution)/shard_map/ppermute | solution.py:72
  17.0 1.1 copy-start.14
  17.0 1.1 copy-start.16
  18.2 2.1 %copy-start.8 = (f32[384,400]{0,1:T(8,128)}, f32[384,400]{0,1:T(8,128)S(1)}, u32[]{:S(2)}) copy-start(f32[384,400]{0,1:T(8,128)S(1)} %fusion.19) | copy-start | bytes 1843204
  18.2 4.6 %copy-start.18 = (s32[1,64]{1,0:T(1,128)S(1)}, s32[1,64]{1,0:T(1,128)}, u32[]{:S(2)}) copy-start(s32[1,64]{1,0:T(1,128)} %param.14) | copy-start | bytes 772
  18.7 0.8 copy-start.4
  20.3 0.7 copy-start.11
  24.2 75.4 %collective-permute-start = (s32[768]{0:T(1024)S(1)}, s32[768]{0:T(1024)S(1)}, u32[]{:S(2)}, u32[]{:S(2)}) collective-permute-start(s32[768]{0:T(1024)S(1)} %reshape.106), channel_id=1, source_target_pairs={{0,1},{1,0},{2,3},{3,2},{4,5},{5,4},{6,7},{7,6},{8,9},{9,8},{10,11... | collective-permute-start | bytes 9224 | tf_op jit(solution)/shard_map/ppermute | solution.py:72
  28.3 0.8 copy-start.10
  74.3 0.9 copy-start
  75.2 5.3 %copy-start.12 = (bf16[384,200]{0,1:T(8,128)(2,1)S(1)}, bf16[384,200]{0,1:T(8,128)(2,1)}, u32[]{:S(2)}) copy-start(bf16[384,200]{0,1:T(8,128)(2,1)} %copy-done.11) | copy-start | bytes 460804
  75.2 3.1 %copy-start.1 = (bf16[16,48,400]{2,1,0:T(8,128)(2,1)S(1)}, bf16[16,48,400]{2,1,0:T(8,128)(2,1)}, u32[]{:S(2)}) copy-start(bf16[16,48,400]{2,1,0:T(8,128)(2,1)} %copy-done) | copy-start | bytes 1843204
  76.8 47.1 %collective-permute-start.2 = (bf16[768,400]{0,1:T(8,128)(2,1)S(1)}, bf16[768,400]{0,1:T(8,128)(2,1)}, u32[]{:S(2)}, u32[]{:S(2)}) collective-permute-start(bf16[768,400]{0,1:T(8,128)(2,1)S(1)} %copy.28), channel_id=1, source_target_pairs={{0,1},{1,0},{2,3},{3,2},{4,5},{5,4},{6,7},{7,6},{8,9},{9,8},{10,11... | collective-permute-start | bytes 1843208 | tf_op jit(solution)/shard_map/ppermute | solution.py:72
  79.9 30.0 %collective-permute-start.1 = (f32[768]{0:T(1024)S(1)}, f32[768]{0:T(1024)S(1)}, u32[]{:S(2)}, u32[]{:S(2)}) collective-permute-start(f32[768]{0:T(1024)S(1)} %divide_negate_fusion), channel_id=1, source_target_pairs={{0,1},{1,0},{2,3},{3,2},{4,5},{5,4},{6,7},{7,6},{8,9},{9,8},{10,11... | collective-permute-start | bytes 9224 | tf_op jit(solution)/shard_map/ppermute | solution.py:72
  80.5 1.8 %copy-start.13 = (bf16[384,200]{0,1:T(8,128)(2,1)S(1)}, bf16[384,200]{0,1:T(8,128)(2,1)}, u32[]{:S(2)}) copy-start(bf16[384,200]{0,1:T(8,128)(2,1)} %copy-done.11) | copy-start | bytes 460804
  82.4 2.3 %copy-start.5 = (f32[384,400]{0,1:T(8,128)S(1)}, f32[384,400]{0,1:T(8,128)}, u32[]{:S(2)}) copy-start(f32[384,400]{0,1:T(8,128)} %copy-done.4) | copy-start | bytes 1843204
  82.4 2.3 %copy-start.9 = (f32[384,400]{0,1:T(8,128)S(1)}, f32[384,400]{0,1:T(8,128)}, u32[]{:S(2)}) copy-start(f32[384,400]{0,1:T(8,128)} %copy-done.8) | copy-start | bytes 1843204
  87.0 19.6 %all-to-all-start.2 = ((f32[32,1,800]{2,1,0:T(1,128)}), f32[32,1,800]{2,1,0:T(1,128)S(1)}, u32[]{:S(2)}, u32[]{:S(2)}) async-start(f32[32,1,800]{2,1,0:T(1,128)} %all_to_all.22), calls=%async_computation.2 | async-start | bytes 229376 | tf_op jit(solution)/shard_map/all_to_all | solution.py:78
  98.2 24.9 %copy-start.15 = (f32[64,400]{1,0:T(8,128)S(1)}, f32[64,400]{1,0:T(8,128)}, u32[]{:S(2)}) copy-start(f32[64,400]{1,0:T(8,128)} %param.9) | copy-start | bytes 307204
  107.4 10.9 %all-to-all-start.3 = ((f32[32,1,800]{2,1,0:T(1,128)}), f32[32,1,800]{2,1,0:T(1,128)S(1)}, u32[]{:S(2)}, u32[]{:S(2)}) async-start(f32[32,1,800]{2,1,0:T(1,128)} %broadcast_in_dim.7), calls=%async_computation.3 | async-start | bytes 229376 | tf_op jit(solution)/shard_map/all_to_all | solution.py:78
  118.3 26.6 %all-to-all-start.1 = ((bf16[16,64,400]{2,1,0:T(8,128)(2,1)}), bf16[16,64,400]{2,1,0:T(8,128)(2,1)S(1)}, u32[]{:S(2)}, u32[]{:S(2)}) async-start(bf16[16,64,400]{2,1,0:T(8,128)(2,1)} %bitcast.7), calls=%async_computation.1 | async-start | bytes 2097152 | tf_op jit(solution)/shard_map/all_to_all | solution.py:78
  125.0 20.1 %copy-start.6 = (f32[384,200]{0,1:T(8,128)S(1)}, f32[384,200]{0,1:T(8,128)}, u32[]{:S(2)}) copy-start(f32[384,200]{0,1:T(8,128)} %get-tuple-element.26) | copy-start | bytes 921604
  125.1 20.1 %copy-start.7 = (f32[384,200]{0,1:T(8,128)S(1)}, f32[384,200]{0,1:T(8,128)}, u32[]{:S(2)}) copy-start(f32[384,200]{0,1:T(8,128)} %get-tuple-element.27) | copy-start | bytes 921604
  145.3 20.8 %collective-permute-start.4 = (f32[448,400]{0,1:T(8,128)S(1)}, f32[448,400]{0,1:T(8,128)S(1)}, u32[]{:S(2)}, u32[]{:S(2)}) collective-permute-start(f32[448,400]{0,1:T(8,128)S(1)} %pad_maximum_fusion.2), channel_id=1, source_target_pairs={{0,1},{1,0},{2,3},{3,2},{4,5},{5,4},{6,7},{7,6},{8,9},{9,8},{10,11... | collective-permute-start | bytes 2150408 | tf_op jit(solution)/shard_map/ppermute | solution.py:72
  170.7 1.9 %copy-start.3 = (f32[2048,400]{0,1:T(8,128)S(1)}, f32[2048,400]{0,1:T(8,128)}, u32[]{:S(2)}) copy-start(f32[2048,400]{0,1:T(8,128)} %param.8) | copy-start | bytes 9830404

commit v3 on v2

--- a/solution.py
+++ b/solution.py
@@ -8,7 +8,6 @@
 
 EPSILON = 1e-06
 LEARN_RATE = 0.3
-NEG_TYPE = jnp.bfloat16
 
 
 def complex_product(factor, other):
@@ -187,11 +186,173 @@
     )(outgoing, located, own_block)
 
 
+def backward_kernel(
+    owners,
+    bits,
+    neg_ref,
+    rel_ref,
+    head_ref,
+    late_out,
+    rel_out,
+    pre,
+    staged,
+    landed,
+    rel_sums,
+    rel_got,
+    pre_send,
+    pre_recv,
+    part_send,
+    part_recv,
+    rel_send,
+    rel_recv,
+    grp_send,
+    grp_recv,
+):
+    me = lax.axis_index("blk")
+    group = lax.axis_index("grp")
+    mate = {"grp": 1 - group}
+    core = lax.rem(me, 2)
+    chip = me // 2
+    sibling = me + 1 - 2 * core
+    chips = owners // 2
+    head_count = head_ref.shape[0]
+    neg_count = neg_ref.shape[1]
+    barrier = pltpu.get_barrier_semaphore()
+
+    def each(low, high, act):
+        def body(step, carry):
+            act(step)
+            return carry
+
+        lax.fori_loop(low, high, body, 0)
+
+    def hello(step):
+        pl.semaphore_signal(
+            barrier,
+            inc=1,
+            device_id={"blk": lax.rem(me + step, owners)},
+            device_id_type=pl.DeviceIdType.MESH,
+        )
+
+    each(1, owners, hello)
+    pl.semaphore_signal(barrier, inc=1, device_id=mate, device_id_type=pl.DeviceIdType.MESH)
+    pl.semaphore_wait(barrier, owners)
+
+    def rel_copy(turn):
+        if turn == 0:
+            device = mate
+        else:
+            bit = 2 ** (turn - 1)
+            device = {"blk": me + bit - 2 * bit * lax.rem(me // bit, 2)}
+        source = rel_ref if turn == 0 else rel_sums.at[turn - 1]
+        return remote(source, rel_got.at[turn], rel_send.at[turn], rel_recv.at[turn], device)
+
+    def rel_turn(turn):
+        rel_copy(turn).wait_recv()
+        source = rel_ref[...] if turn == 0 else rel_sums[turn - 1]
+        if turn < bits:
+            rel_sums[turn] = source + rel_got[turn]
+            rel_copy(turn + 1).start()
+        else:
+            rel_out[...] = source + rel_got[turn]
+
+    def pre_copy(step):
+        there = lax.rem(chip + step, chips)
+        return remote(
+            neg_ref.at[2 * there + 1 - core],
+            pre.at[there],
+            pre_send.at[step],
+            pre_recv.at[step],
+            {"blk": sibling},
+        )
+
+    def part_copy(step):
+        there = lax.rem(chip + step, chips)
+        return remote(
+            staged.at[there],
+            landed.at[chip],
+            part_send.at[step],
+            part_recv.at[step],
+            {"blk": 2 * there + core},
+        )
+
+    head_rows = late_out.at[group, pl.ds(0, head_count)]
+    head_copy = remote(head_ref, head_rows, grp_send.at[0], grp_recv.at[0], mate)
+    sum_rows = late_out.at[group, pl.ds(head_count, neg_count)]
+    sum_copy = remote(sum_rows, sum_rows, grp_send.at[1], grp_recv.at[1], mate)
+
+    rel_copy(0).start()
+    each(0, chips, lambda step: pre_copy(step).start())
+    head_copy.start()
+    late_out[group, pl.ds(0, head_count)] = head_ref[...]
+    rel_turn(0)
+
+    def part(step):
+        there = lax.rem(chip + step, chips)
+        pre_copy(step).wait_recv()
+        staged[there] = (neg_ref[2 * there + core] + pre[there]).astype(jnp.bfloat16)
+        part_copy(step).start()
+
+    each(1, chips, part)
+    for turn in range(1, bits + 1):
+        rel_turn(turn)
+    pre_copy(0).wait_recv()
+    late_out[group, pl.ds(head_count, neg_count)] = neg_ref[me] + pre[chip]
+
+    def add(step):
+        part_copy(step).wait_recv()
+        origin = lax.rem(chip - step + chips, chips)
+        late_out[group, pl.ds(head_count, neg_count)] += landed[origin].astype(jnp.float32)
+
+    each(1, chips, add)
+    sum_copy.start()
+    for turn in range(bits + 1):
+        rel_copy(turn).wait_send()
+    each(0, chips, lambda step: pre_copy(step).wait_send())
+    each(1, chips, lambda step: part_copy(step).wait_send())
+    head_copy.wait()
+    sum_copy.wait()
+
+
+def backward_exchange(neg_parts, rel_local, grad_head):
+    owners, neg_count, width = neg_parts.shape
+    bits = owners.bit_length() - 1
+    chips = owners // 2
+    vmem = pl.BlockSpec(memory_space=pltpu.VMEM)
+    late_count = grad_head.shape[0] + neg_count
+    return pl.pallas_call(
+        functools.partial(backward_kernel, owners, bits),
+        out_shape=(
+            jax.ShapeDtypeStruct((2, late_count, width), jnp.float32),
+            jax.ShapeDtypeStruct(rel_local.shape, jnp.float32),
+        ),
+        in_specs=[vmem] * 3,
+        out_specs=(vmem,) * 2,
+        scratch_shapes=[
+            pltpu.VMEM((chips, neg_count, width), jnp.float32),
+            pltpu.VMEM((chips, neg_count, width), jnp.bfloat16),
+            pltpu.VMEM((chips, neg_count, width), jnp.bfloat16),
+            pltpu.VMEM((bits + 1,) + rel_local.shape, jnp.float32),
+            pltpu.VMEM((bits + 1,) + rel_local.shape, jnp.float32),
+            pltpu.SemaphoreType.DMA((chips,)),
+            pltpu.SemaphoreType.DMA((chips,)),
+            pltpu.SemaphoreType.DMA((chips,)),
+            pltpu.SemaphoreType.DMA((chips,)),
+            pltpu.SemaphoreType.DMA((bits + 1,)),
+            pltpu.SemaphoreType.DMA((bits + 1,)),
+            pltpu.SemaphoreType.DMA((2,)),
+            pltpu.SemaphoreType.DMA((2,)),
+        ],
+        compiler_params=pltpu.CompilerParams(
+            collective_id=2, has_side_effects=True, vmem_limit_bytes=48 * 2**20
+        ),
+    )(neg_parts, rel_local, grad_head)
+
+
 def per_device(
     entities, relations, head_row, relation_id, tail_owner, tail_row, negative_rows, edge_count
 ):
     owners = lax.axis_size("blk")
-    devices = owners * lax.axis_size("grp")
     edge_total = head_row.shape[0]
     ent_count, row_width = entities.shape
     neg_count = negative_rows.shape[1]
@@ -238,8 +399,6 @@
     nweight = (neg_scale * live[:, None] * jax.nn.sigmoid(scores)).astype(jnp.bfloat16)
     neg_query = jnp.dot(nweight, piece, preferred_element_type=jnp.float32)
     neg_grads = jnp.dot(nweight.T, query_bf, preferred_element_type=jnp.float32)
-    neg_parts = deal(neg_grads.astype(NEG_TYPE).reshape(owners, neg_count, row_width), "blk")
-    neg_sum = jnp.sum(neg_parts.astype(jnp.float32), axis=0)
 
     tail_bf = pick(slot_hot, arrived.reshape(owners * capacity, row_width))
     tail_f = tail_bf.astype(jnp.float32)
@@ -247,10 +406,10 @@
     grad_query = weight[:, None] * tail_f + neg_query
     grad_head, grad_rel = complex_grads(grad_query, head_f, rel_rows)
     rel_local = jnp.dot(rel_onehot.T, grad_rel, precision=lax.Precision.HIGHEST)
-    rel_parts = deal(rel_local.reshape(devices, -1), ("blk", "grp"))
-    rel_share = jnp.sum(rel_parts, axis=0)
-    rel_total = deal(jnp.broadcast_to(rel_share[None], rel_parts.shape), ("blk", "grp"))
-    new_relations = adagrad(relations, rel_total.reshape(rel_count, row_width))
+    late, rel_total = backward_exchange(
+        neg_grads.reshape(owners, neg_count, row_width), rel_local, grad_head
+    )
+    new_relations = adagrad(relations, rel_total)
 
     returned_f = returned.astype(jnp.float32)
     owner_weight = -jax.nn.sigmoid(-jnp.sum(returned_f * located.astype(jnp.float32), axis=1))
@@ -259,7 +418,7 @@
     tail_grads = tail_weights[:, None] * swap(returned).astype(jnp.float32)
     entity_grads = spread(tail_rows, ent_count, tail_grads)
     late_rows = jnp.concatenate([head_row, negative_rows[0]])
-    late = swap(jnp.concatenate([grad_head, neg_sum], axis=0))
+    late = late.reshape(-1, row_width)
     entity_grads = entity_grads + spread(swap(late_rows), ent_count, late)
     new_entities = adagrad(entities, entity_grads)
     return (new_entities, new_relations)

time: 176 us -> 144 us (0.82)
  waiting for transfers between devices: 46.7 us -> 0.01 us
  Pallas kernels: 45.2 us -> 86.2 us
  starting transfers between devices: 29.6 us -> 11.5 us
  other arithmetic: 16.3 us -> 12.6 us
  local copies, waits for them, and re-layouts: 8.18 us -> 5.5 us
    pallas_call x0 -> x1, Pallas kernels: none -> 41 us  [backward_exchange(): pl.pallas_call(functools.partial(backward_kernel, owners, bits), out_shap...]
    all_to_all x4 -> x1, waiting for transfers between devices: 33.8 us -> 0.01 us  [deal(): return lax.all_to_all(blocks, axes, split_axis=0, concat_axis=0, tiled=True)]
    all_to_all x4 -> x1, starting transfers between devices: 25 us -> 7.39 us  [deal(): return lax.all_to_all(blocks, axes, split_axis=0, concat_axis=0, tiled=True)]
    ppermute x5 -> x4, waiting for transfers between devices: 12.9 us -> 0.01 us  [swap(): other = lax.ppermute(own, 'grp', pairs)]
    ppermute x5 -> x4, starting transfers between devices: 4.61 us -> 4.13 us  [swap(): other = lax.ppermute(own, 'grp', pairs)]
  transfers between devices with their start and end apart: 9 -> 5, of which waited for: 4 -> 0; matrix products, arithmetic and copies ran while one was open for 19% -> 18% of each run, Pallas kernels for 26% -> 60%
where the time goes in v3:
time: 144 us
  Pallas kernels  86.2 us (60%)
  matrix products  26.2 us (18%)
  other arithmetic  12.6 us (9%)
  starting transfers between devices  11.5 us (8%)
  local copies, waits for them, and re-layouts  5.5 us (4%)
  between operations  1.82 us (1%)
    pallas_call x1, Pallas kernels, forward_exchange(): pl.pallas_call(functools.partial(forward_kernel, owners), out_shape=(jax....  45.2 us
    pallas_call x1, Pallas kernels, backward_exchange(): pl.pallas_call(functools.partial(backward_kernel, owners, bits), out_shap...  41 us
    dot_general x2, matrix products, spread(): lax.dot_general(hot, both, (((0,), (0,)), ((), ())), preferred_element_ty...  10 us
    dot_general x4, matrix products, pick(): jnp.dot(hot, table, preferred_element_type=jnp.float32).astype(jnp.bfloat16)  8.81 us
    all_to_all x1, starting transfers between devices, deal(): return lax.all_to_all(blocks, axes, split_axis=0, concat_axis=0, tiled=True)  7.39 us
    ppermute x4, starting transfers between devices, swap(): other = lax.ppermute(own, 'grp', pairs)  4.13 us
    unnamed x28, local copies, waits for them, and re-layouts  3.45 us
    sub x2, other arithmetic, adagrad(): return table - LEARN_RATE * table_grads / (jnp.sqrt(square_mean) + EPSILON)  3.2 us
  transfers between devices with their start and end apart: 5, of which 0 were waited for; matrix products, arithmetic and copies ran while one was open for 18% of the time, Pallas kernels for 60%

profile of v3, /device:TPU:0, one launch (start us, length us, event | category | flops | bytes accessed | tf_op | source)
XLA Modules:
  0.0 143.8 jit_solution(5663245042548175967)
XLA Ops:
  0.6 0.0 copy-start.12
  0.6 0.0 copy-start.2
  1.4 0.9 reduce
  2.3 0.2 fusion.21
  2.6 0.7 add_reduce_fusion
  3.3 0.7 select_add_fusion
  4.0 0.2 select_reduce_fusion
  4.2 0.7 sub.28
  4.8 7.4 %all-to-all-start = ((s32[16,1,48]{2,1,0:T(1,128)}), s32[16,1,48]{2,1,0:T(1,128)S(1)}, u32[]{:S(2)}, u32[]{:S(2)}) async-start(s32[16,1,48]{2,1,0:T(1,128)} %sub.28), calls=%async_computation | async-start | bytes 16384 | tf_op jit(solution)/shard_map/all_to_all | solution.py:77
  12.2 0.7 pad_add_fusion.2
  12.9 1.5 %collective-permute-start.3 = (s32[448]{0:T(512)S(1)}, s32[448]{0:T(512)S(1)}, u32[]{:S(2)}, u32[]{:S(2)}) collective-permute-start(s32[448]{0:T(512)S(1)} %pad_add_fusion.2), channel_id=1, source_target_pairs={{0,1},{1,0},{2,3},{3,2},{4,5},{5,4},{6,7},{7,6},{8,9},{9,8},{10,11... | collective-permute-start | bytes 5384 | tf_op jit(solution)/shard_map/ppermute | solution.py:71
  14.4 2.6 %convolution_convert_fusion.2.own_ref = bf16[64,400]{1,0:T(8,128)(2,1)S(1)} fusion(s32[64]{0:T(128)} %bitcast.27, f32[2048,400]{0,1:T(8,128)} %param.8), kind=kOutput, calls=%fused_computation.42 | convolution fusion | flops 105833472 | bytes 3328256 | tf_op jit(solution)/shard_map/dot_general | solution.py:55
  17.0 0.0 copy-start.9
  17.0 0.0 copy-start.11
  17.1 1.0 fusion.19
  18.1 0.5 fusion.29
  18.6 0.9 copy-done.4
  19.5 1.1 subtract_convert_fusion
  20.6 1.9 %convolution_convert_fusion = bf16[768,400]{0,1:T(8,128)(2,1)S(1)} fusion(s32[384]{0:T(512)S(1)} %add_reduce_fusion, bf16[384,200]{1,0:T(8,128)(2,1)} %get-tuple-element.21, bf16[384,200]{1,0:T(8,128)(2,1)} %get-tuple-element.20), kind=kOutput, calls=%fused_computation.32 | convolution fusion | flops 237146112 | bytes 923136 | tf_op jit(solution)/shard_map/dot_general | solution.py:386
  22.5 0.3 copy.34
  22.7 0.0 collective-permute-done.3
  22.8 0.1 pad_add_fusion.1
  22.9 0.0 all-to-all-done
  22.9 0.5 broadcast.106
  23.4 0.7 reduce.6
  24.0 0.1 reshape.94
  24.1 0.5 collective-permute-start
  24.7 3.6 %fusion.17 = bf16[768,400]{0,1:T(8,128)(2,1)S(1)} fusion(s32[768]{0:T(1024)S(1)} %reshape.94, f32[2048,400]{0,1:T(8,128)} %param.8), kind=kOutput, calls=%fused_computation.31 | convolution fusion | flops 1260990464 | bytes 3894272 | tf_op jit(solution)/shard_map/dot_general | solution.py:55
  28.3 0.3 copy.35
  28.6 0.5 copy-done.8
  29.1 45.2 %shard_map.95 = (bf16[16,48,400]{2,1,0:T(8,128)(2,1)S(1)}, bf16[16,48,400]{2,1,0:T(8,128)(2,1)S(1)}, bf16[16,64,400]{2,1,0:T(8,128)(2,1)S(1)}) custom-call(bf16[16,48,400]{2,1,0:T(8,128)(2,1)S(1)} %bitcast.20, bf16[16,48,400]{2,1,0:T(8,128)(2,1)S(1)} %bitcast.21, bf16[64,400]{1,0:T(8,128)(2,1)S(1)} %convolution_convert_fusion.2.own_ref), custom_call_target="tpu_custom_call" | custom-call | tf_op jit(solution)/shard_map/pallas_call | solution.py:168
  74.3 0.0 copy-start
  74.3 0.9 copy-done
  75.1 0.2 copy.36
  75.4 1.3 multiply_reduce_fusion.1
  76.7 1.5 %collective-permute-start.2 = (bf16[768,400]{0,1:T(8,128)(2,1)S(1)}, bf16[768,400]{0,1:T(8,128)(2,1)S(1)}, u32[]{:S(2)}, u32[]{:S(2)}) collective-permute-start(bf16[768,400]{0,1:T(8,128)(2,1)S(1)} %copy.36), channel_id=1, source_target_pairs={{0,1},{1,0},{2,3},{3,2},{4,5},{5,4},{6,7},{7,6},{8,9},{9,8},{10,11... | collective-permute-start | bytes 1843208 | tf_op jit(solution)/shard_map/ppermute | solution.py:71
  78.2 0.5 collective-permute-start.1
  78.8 0.0 copy-done.1
  78.8 1.6 %multiply_reduce_fusion.2 = (f32[384]{0:T(512)S(1)}, f32[384,400]{1,0:T(8,128)S(1)}) fusion(bf16[384,200]{1,0:T(8,128)(2,1)} %get-tuple-element.21, bf16[384,200]{1,0:T(8,128)(2,1)} %get-tuple-element.20, bf16[768,400]{1,0:T(8,128)(2,1)S(1)} %bitcast.25, s32[384]{0:T(512)S(1)} %add_reduce_fusion), kind=kOutput, calls=%fused_computation.50 | convolution fusion | flops 237452928 | bytes 1539072 | tf_op jit(solution)/shard_map/dot_general | solution.py:55
  80.4 1.8 %multiply_convert_fusion = bf16[384,1024]{1,0:T(8,128)(2,1)S(1)} fusion(bf16[1024,400]{1,0:T(8,128)(2,1)S(1)} %bitcast.22, f32[384]{0:T(512)S(1)} %get-tuple-element.37, bf16[384,200]{1,0:T(8,128)(2,1)} %get-tuple-element.21, bf16[384,200]{1,0:T(8,128)(2,1)} %get-tuple-element.20), kind=kOutput, calls=%fused_computation.29 | convolution fusion | flops 317153280 | bytes 1914368 | tf_op jit(solution)/shard_map/dot_general | solution.py:398
  82.2 1.8 %fusion.40 = f32[1024,400]{1,0:T(8,128)S(1)} fusion(bf16[384,1024]{1,0:T(8,128)(2,1)S(1)} %multiply_convert_fusion, bf16[384,200]{1,0:T(8,128)(2,1)} %get-tuple-element.21, bf16[384,200]{1,0:T(8,128)(2,1)} %get-tuple-element.20), kind=kOutput, calls=%fused_computation.99 | convolution fusion | flops 315187200 | bytes 2732032 | tf_op jit(solution)/shard_map/dot_general | solution.py:401
  84.1 0.6 convolution_add_fusion
  84.6 0.5 copy-done.5
  85.2 0.2 copy-done.7
  85.4 0.4 multiply_add_fusion
  85.8 0.2 pad_maximum_fusion.1.head_ref
  86.0 0.6 fusion.22.rel_ref
  86.6 41.0 %shard_map.96 = (f32[2,448,400]{2,1,0:T(8,128)S(1)}, f32[64,400]{1,0:T(8,128)S(1)}) custom-call(f32[16,64,400]{2,1,0:T(8,128)S(1)} %bitcast.19, f32[64,400]{1,0:T(8,128)S(1)} %fusion.22.rel_ref, f32[384,400]{1,0:T(8,128)S(1)} %pad_maximum_fusion.1.head_ref), custom_call_target="tpu_custom_call" | custom-call | tf_op jit(solution)/shard_map/pallas_call | solution.py:323
  127.6 0.3 reduce-precision_convert_fusion.1
  127.9 0.1 multiply_reduce_fusion.3
  128.0 0.0 copy-start.10
  128.0 4.2 %fusion.1 = f32[2048,800]{0,1:T(8,128)S(1)} fusion(s32[896]{0:T(1024)S(1)} %pad_add_fusion.1, bf16[896,400]{1,0:T(8,128)(2,1)S(1)} %get-tuple-element.15, bf16[896,400]{1,0:T(8,128)(2,1)S(1)} %get-tuple-element.14), kind=kOutput, calls=%fused_computation.3 | convolution fusion | flops 2940715008 | bytes 7990784 | tf_op jit(solution)/shard_map/dot_general | solution.py:62
  132.2 0.0 copy-done.10
  132.2 0.7 divide_subtract_fusion.1
  133.0 0.0 collective-permute-done
  133.0 0.0 collective-permute-done.1
  133.0 0.0 collective-permute-done.2
  133.0 0.1 broadcast_select_fusion.1
  133.1 0.4 reduce-precision_convert_fusion
  133.5 5.9 %fusion = f32[2048,800]{0,1:T(8,128)S(1)} fusion(s32[1536]{0:T(1024)S(1)} %pad_add_fusion, bf16[1536,400]{0,1:T(8,128)(2,1)S(1)} %get-tuple-element.23, bf16[1536,400]{0,1:T(8,128)(2,1)S(1)} %get-tuple-element.22), kind=kOutput, calls=%fused_computation.1 | convolution fusion | flops 5041225728 | bytes 9017344 | tf_op jit(solution)/shard_map/dot_general | solution.py:62
  139.4 0.0 copy-start.3
  139.4 1.6 %multiply_reduce_fusion = (f32[2048]{0:T(1024)S(1)}, f32[2048,400]{0,1:T(8,128)S(1)}) fusion(f32[2048,800]{0,1:T(8,128)S(1)} %fusion.1, f32[2048,800]{0,1:T(8,128)S(1)} %fusion), kind=kLoop, calls=%fused_computation.14 | loop fusion | flops 4093952 | bytes 16392192 | tf_op jit(solution)/shard_map/reduce_sum | solution.py:46
  141.0 0.3 copy-done.3
  141.3 2.5 %divide_subtract_fusion = f32[2048,400]{0,1:T(8,128)} fusion(f32[2048,400]{0,1:T(8,128)S(1)} %copy-done.3, f32[2048,400]{0,1:T(8,128)S(1)} %get-tuple-element.13, f32[2048]{0:T(1024)S(1)} %sqrt_add_fusion), kind=kLoop, calls=%fused_computation.13 | loop fusion | flops 2457600 | bytes 9838592 | tf_op jit(solution)/shard_map/sub | solution.py:47
  (24 shorter events, 0.1 us)
Async XLA Ops:
  0.6 16.4 %copy-start.12 = (s32[384]{0:T(512)S(1)}, s32[384]{0:T(512)}, u32[]{:S(2)}) copy-start(s32[384]{0:T(512)} %param.10) | copy-start | bytes 4612
  0.6 16.4 %copy-start.2 = (f32[2048,400]{0,1:T(8,128)S(1)}, f32[2048,400]{0,1:T(8,128)}, u32[]{:S(2)}) copy-start(f32[2048,400]{0,1:T(8,128)} %param.8) | copy-start | bytes 9830404
  4.8 18.0 %all-to-all-start = ((s32[16,1,48]{2,1,0:T(1,128)}), s32[16,1,48]{2,1,0:T(1,128)S(1)}, u32[]{:S(2)}, u32[]{:S(2)}) async-start(s32[16,1,48]{2,1,0:T(1,128)} %sub.28), calls=%async_computation | async-start | bytes 16384 | tf_op jit(solution)/shard_map/all_to_all | solution.py:77
  12.9 9.8 %collective-permute-start.3 = (s32[448]{0:T(512)S(1)}, s32[448]{0:T(512)S(1)}, u32[]{:S(2)}, u32[]{:S(2)}) collective-permute-start(s32[448]{0:T(512)S(1)} %pad_add_fusion.2), channel_id=1, source_target_pairs={{0,1},{1,0},{2,3},{3,2},{4,5},{5,4},{6,7},{7,6},{8,9},{9,8},{10,11... | collective-permute-start | bytes 5384 | tf_op jit(solution)/shard_map/ppermute | solution.py:71
  17.0 1.1 copy-start.9
  17.0 1.1 copy-start.11
  18.1 2.5 %copy-start.6 = (f32[384,400]{1,0:T(8,128)}, f32[384,400]{1,0:T(8,128)S(1)}, u32[]{:S(2)}) copy-start(f32[384,400]{1,0:T(8,128)S(1)} %fusion.19) | copy-start | bytes 1843204
  18.6 0.9 copy-start.4
  19.5 3.2 %copy-start.13 = (s32[1,64]{1,0:T(1,128)S(1)}, s32[1,64]{1,0:T(1,128)}, u32[]{:S(2)}) copy-start(s32[1,64]{1,0:T(1,128)} %param.14) | copy-start | bytes 772
  24.1 108.8 %collective-permute-start = (s32[768]{0:T(1024)S(1)}, s32[768]{0:T(1024)S(1)}, u32[]{:S(2)}, u32[]{:S(2)}) collective-permute-start(s32[768]{0:T(1024)S(1)} %reshape.94), channel_id=1, source_target_pairs={{0,1},{1,0},{2,3},{3,2},{4,5},{5,4},{6,7},{7,6},{8,9},{9,8},{10,11... | collective-permute-start | bytes 9224 | tf_op jit(solution)/shard_map/ppermute | solution.py:71
  28.3 0.8 copy-start.8
  74.3 0.9 copy-start
  75.1 3.6 %copy-start.1 = (bf16[16,48,400]{2,1,0:T(8,128)(2,1)S(1)}, bf16[16,48,400]{2,1,0:T(8,128)(2,1)}, u32[]{:S(2)}) copy-start(bf16[16,48,400]{2,1,0:T(8,128)(2,1)} %copy-done) | copy-start | bytes 1843204
  76.7 56.4 %collective-permute-start.2 = (bf16[768,400]{0,1:T(8,128)(2,1)S(1)}, bf16[768,400]{0,1:T(8,128)(2,1)S(1)}, u32[]{:S(2)}, u32[]{:S(2)}) collective-permute-start(bf16[768,400]{0,1:T(8,128)(2,1)S(1)} %copy.36), channel_id=1, source_target_pairs={{0,1},{1,0},{2,3},{3,2},{4,5},{5,4},{6,7},{7,6},{8,9},{9,8},{10,11... | collective-permute-start | bytes 1843208 | tf_op jit(solution)/shard_map/ppermute | solution.py:71
  78.2 54.8 %collective-permute-start.1 = (f32[768]{0:T(1024)S(1)}, f32[768]{0:T(1024)S(1)}, u32[]{:S(2)}, u32[]{:S(2)}) collective-permute-start(f32[768]{0:T(1024)S(1)} %divide_negate_fusion), channel_id=1, source_target_pairs={{0,1},{1,0},{2,3},{3,2},{4,5},{5,4},{6,7},{7,6},{8,9},{9,8},{10,11... | collective-permute-start | bytes 9224 | tf_op jit(solution)/shard_map/ppermute | solution.py:71
  84.0 1.1 copy-start.5
  84.1 1.4 copy-start.7
  128.0 4.2 %copy-start.10 = (f32[64,400]{1,0:T(8,128)S(1)}, f32[64,400]{1,0:T(8,128)}, u32[]{:S(2)}) copy-start(f32[64,400]{1,0:T(8,128)} %param.9) | copy-start | bytes 307204
  139.4 1.9 %copy-start.3 = (f32[2048,400]{0,1:T(8,128)S(1)}, f32[2048,400]{0,1:T(8,128)}, u32[]{:S(2)}) copy-start(f32[2048,400]{0,1:T(8,128)} %param.8) | copy-start | bytes 9830404

commit v4 on v3

--- a/solution.py
+++ b/solution.py
@@ -239,10 +239,10 @@
     pl.semaphore_wait(barrier, owners)
 
     def rel_copy(turn):
-        if turn == 0:
+        if turn == bits:
             device = mate
         else:
-            bit = 2 ** (turn - 1)
+            bit = 2**turn
             device = {"blk": me + bit - 2 * bit * lax.rem(me // bit, 2)}
         source = rel_ref if turn == 0 else rel_sums.at[turn - 1]
         return remote(source, rel_got.at[turn], rel_send.at[turn], rel_recv.at[turn], device)

time: 144 us -> 143 us (level)
  no operation moved by 1% of the time
where the time goes in v4:
time: 143 us; the launch traced here: 142 us
  Pallas kernels  84.9 us (59%)
  matrix products  26.2 us (18%)
  other arithmetic  12.6 us (9%)
  starting transfers between devices  11.5 us (8%)
  local copies, waits for them, and re-layouts  5.5 us (4%)
  between operations  1.82 us (1%)
    pallas_call x1, Pallas kernels, forward_exchange(): pl.pallas_call(functools.partial(forward_kernel, owners), out_shape=(jax....  45.2 us
    pallas_call x1, Pallas kernels, backward_exchange(): pl.pallas_call(functools.partial(backward_kernel, owners, bits), out_shap...  39.7 us
    dot_general x2, matrix products, spread(): lax.dot_general(hot, both, (((0,), (0,)), ((), ())), preferred_element_ty...  10 us
    dot_general x4, matrix products, pick(): jnp.dot(hot, table, preferred_element_type=jnp.float32).astype(jnp.bfloat16)  8.81 us
    all_to_all x1, starting transfers between devices, deal(): return lax.all_to_all(blocks, axes, split_axis=0, concat_axis=0, tiled=True)  7.39 us
    ppermute x4, starting transfers between devices, swap(): other = lax.ppermute(own, 'grp', pairs)  4.13 us
    unnamed x28, local copies, waits for them, and re-layouts  3.45 us
    sub x2, other arithmetic, adagrad(): return table - LEARN_RATE * table_grads / (jnp.sqrt(square_mean) + EPSILON)  3.2 us
  transfers between devices with their start and end apart: 5, of which 0 were waited for; matrix products, arithmetic and copies ran while one was open for 18% of the time, Pallas kernels for 60%

profile of v4, /device:TPU:0, one launch (start us, length us, event | category | flops | bytes accessed | tf_op | source)
XLA Modules:
  0.0 142.5 jit_solution(8652178369251545619)
XLA Ops:
  0.6 0.0 copy-start.12
  0.6 0.0 copy-start.2
  1.4 0.9 reduce
  2.3 0.2 fusion.21
  2.6 0.7 add_reduce_fusion
  3.3 0.7 select_add_fusion
  4.0 0.2 select_reduce_fusion
  4.2 0.7 sub.28
  4.8 7.4 %all-to-all-start = ((s32[16,1,48]{2,1,0:T(1,128)}), s32[16,1,48]{2,1,0:T(1,128)S(1)}, u32[]{:S(2)}, u32[]{:S(2)}) async-start(s32[16,1,48]{2,1,0:T(1,128)} %sub.28), calls=%async_computation | async-start | bytes 16384 | tf_op jit(solution)/shard_map/all_to_all | solution.py:77
  12.2 0.7 pad_add_fusion.2
  12.9 1.5 %collective-permute-start.3 = (s32[448]{0:T(512)S(1)}, s32[448]{0:T(512)S(1)}, u32[]{:S(2)}, u32[]{:S(2)}) collective-permute-start(s32[448]{0:T(512)S(1)} %pad_add_fusion.2), channel_id=1, source_target_pairs={{0,1},{1,0},{2,3},{3,2},{4,5},{5,4},{6,7},{7,6},{8,9},{9,8},{10,11... | collective-permute-start | bytes 5384 | tf_op jit(solution)/shard_map/ppermute | solution.py:71
  14.4 2.6 %convolution_convert_fusion.2.own_ref = bf16[64,400]{1,0:T(8,128)(2,1)S(1)} fusion(s32[64]{0:T(128)} %bitcast.27, f32[2048,400]{0,1:T(8,128)} %param.8), kind=kOutput, calls=%fused_computation.42 | convolution fusion | flops 105833472 | bytes 3328256 | tf_op jit(solution)/shard_map/dot_general | solution.py:55
  17.0 0.0 copy-done.12
  17.0 0.0 copy-done.2
  17.0 0.0 copy-start.9
  17.0 0.0 copy-start.11
  17.1 1.0 fusion.19
  18.1 0.5 fusion.29
  18.6 0.9 copy-done.4
  19.5 1.1 subtract_convert_fusion
  20.6 1.9 %convolution_convert_fusion = bf16[768,400]{0,1:T(8,128)(2,1)S(1)} fusion(s32[384]{0:T(512)S(1)} %add_reduce_fusion, bf16[384,200]{1,0:T(8,128)(2,1)} %get-tuple-element.21, bf16[384,200]{1,0:T(8,128)(2,1)} %get-tuple-element.20), kind=kOutput, calls=%fused_computation.32 | convolution fusion | flops 237146112 | bytes 923136 | tf_op jit(solution)/shard_map/dot_general | solution.py:386
  22.5 0.3 copy.34
  22.7 0.0 collective-permute-done.3
  22.8 0.1 pad_add_fusion.1
  22.9 0.0 all-to-all-done
  22.9 0.5 broadcast.106
  23.4 0.7 reduce.6
  24.0 0.1 reshape.94
  24.1 0.5 collective-permute-start
  24.7 3.6 %fusion.17 = bf16[768,400]{0,1:T(8,128)(2,1)S(1)} fusion(s32[768]{0:T(1024)S(1)} %reshape.94, f32[2048,400]{0,1:T(8,128)} %param.8), kind=kOutput, calls=%fused_computation.31 | convolution fusion | flops 1260990464 | bytes 3894272 | tf_op jit(solution)/shard_map/dot_general | solution.py:55
  28.3 0.3 copy.35
  28.6 0.5 copy-done.8
  29.1 45.2 %shard_map.95 = (bf16[16,48,400]{2,1,0:T(8,128)(2,1)S(1)}, bf16[16,48,400]{2,1,0:T(8,128)(2,1)S(1)}, bf16[16,64,400]{2,1,0:T(8,128)(2,1)S(1)}) custom-call(bf16[16,48,400]{2,1,0:T(8,128)(2,1)S(1)} %bitcast.20, bf16[16,48,400]{2,1,0:T(8,128)(2,1)S(1)} %bitcast.21, bf16[64,400]{1,0:T(8,128)(2,1)S(1)} %convolution_convert_fusion.2.own_ref), custom_call_target="tpu_custom_call" | custom-call | tf_op jit(solution)/shard_map/pallas_call | solution.py:168
  74.3 0.0 copy-start
  74.3 0.9 copy-done
  75.1 0.2 copy.36
  75.4 1.3 multiply_reduce_fusion.1
  76.7 1.5 %collective-permute-start.2 = (bf16[768,400]{0,1:T(8,128)(2,1)S(1)}, bf16[768,400]{0,1:T(8,128)(2,1)S(1)}, u32[]{:S(2)}, u32[]{:S(2)}) collective-permute-start(bf16[768,400]{0,1:T(8,128)(2,1)S(1)} %copy.36), channel_id=1, source_target_pairs={{0,1},{1,0},{2,3},{3,2},{4,5},{5,4},{6,7},{7,6},{8,9},{9,8},{10,11... | collective-permute-start | bytes 1843208 | tf_op jit(solution)/shard_map/ppermute | solution.py:71
  78.2 0.5 collective-permute-start.1
  78.8 1.6 %multiply_reduce_fusion.2 = (f32[384]{0:T(512)S(1)}, f32[384,400]{1,0:T(8,128)S(1)}) fusion(bf16[384,200]{1,0:T(8,128)(2,1)} %get-tuple-element.21, bf16[384,200]{1,0:T(8,128)(2,1)} %get-tuple-element.20, bf16[768,400]{1,0:T(8,128)(2,1)S(1)} %bitcast.25, s32[384]{0:T(512)S(1)} %add_reduce_fusion), kind=kOutput, calls=%fused_computation.50 | convolution fusion | flops 237452928 | bytes 1539072 | tf_op jit(solution)/shard_map/dot_general | solution.py:55
  80.4 1.8 %multiply_convert_fusion = bf16[384,1024]{1,0:T(8,128)(2,1)S(1)} fusion(bf16[1024,400]{1,0:T(8,128)(2,1)S(1)} %bitcast.22, f32[384]{0:T(512)S(1)} %get-tuple-element.37, bf16[384,200]{1,0:T(8,128)(2,1)} %get-tuple-element.21, bf16[384,200]{1,0:T(8,128)(2,1)} %get-tuple-element.20), kind=kOutput, calls=%fused_computation.29 | convolution fusion | flops 317153280 | bytes 1914368 | tf_op jit(solution)/shard_map/dot_general | solution.py:398
  82.2 1.8 %fusion.40 = f32[1024,400]{1,0:T(8,128)S(1)} fusion(bf16[384,1024]{1,0:T(8,128)(2,1)S(1)} %multiply_convert_fusion, bf16[384,200]{1,0:T(8,128)(2,1)} %get-tuple-element.21, bf16[384,200]{1,0:T(8,128)(2,1)} %get-tuple-element.20), kind=kOutput, calls=%fused_computation.99 | convolution fusion | flops 315187200 | bytes 2732032 | tf_op jit(solution)/shard_map/dot_general | solution.py:401
  84.1 0.6 convolution_add_fusion
  84.6 0.5 copy-done.5
  85.2 0.2 copy-done.7
  85.4 0.4 multiply_add_fusion
  85.8 0.2 pad_maximum_fusion.1.head_ref
  86.0 0.6 fusion.22.rel_ref
  86.6 39.7 %shard_map.96 = (f32[2,448,400]{2,1,0:T(8,128)S(1)}, f32[64,400]{1,0:T(8,128)S(1)}) custom-call(f32[16,64,400]{2,1,0:T(8,128)S(1)} %bitcast.19, f32[64,400]{1,0:T(8,128)S(1)} %fusion.22.rel_ref, f32[384,400]{1,0:T(8,128)S(1)} %pad_maximum_fusion.1.head_ref), custom_call_target="tpu_custom_call" | custom-call | tf_op jit(solution)/shard_map/pallas_call | solution.py:323
  126.3 0.3 reduce-precision_convert_fusion.1
  126.6 0.1 multiply_reduce_fusion.3
  126.7 0.0 copy-start.10
  126.7 4.2 %fusion.1 = f32[2048,800]{0,1:T(8,128)S(1)} fusion(s32[896]{0:T(1024)S(1)} %pad_add_fusion.1, bf16[896,400]{1,0:T(8,128)(2,1)S(1)} %get-tuple-element.15, bf16[896,400]{1,0:T(8,128)(2,1)S(1)} %get-tuple-element.14), kind=kOutput, calls=%fused_computation.3 | convolution fusion | flops 2940715008 | bytes 7990784 | tf_op jit(solution)/shard_map/dot_general | solution.py:62
  130.9 0.7 divide_subtract_fusion.1
  131.6 0.0 collective-permute-done
  131.7 0.0 collective-permute-done.1
  131.7 0.0 collective-permute-done.2
  131.7 0.1 broadcast_select_fusion.1
  131.8 0.4 reduce-precision_convert_fusion
  132.2 5.9 %fusion = f32[2048,800]{0,1:T(8,128)S(1)} fusion(s32[1536]{0:T(1024)S(1)} %pad_add_fusion, bf16[1536,400]{0,1:T(8,128)(2,1)S(1)} %get-tuple-element.23, bf16[1536,400]{0,1:T(8,128)(2,1)S(1)} %get-tuple-element.22), kind=kOutput, calls=%fused_computation.1 | convolution fusion | flops 5041225728 | bytes 9017344 | tf_op jit(solution)/shard_map/dot_general | solution.py:62
  138.1 0.0 copy-start.3
  138.1 1.6 %multiply_reduce_fusion = (f32[2048]{0:T(1024)S(1)}, f32[2048,400]{0,1:T(8,128)S(1)}) fusion(f32[2048,800]{0,1:T(8,128)S(1)} %fusion.1, f32[2048,800]{0,1:T(8,128)S(1)} %fusion), kind=kLoop, calls=%fused_computation.14 | loop fusion | flops 4093952 | bytes 16392192 | tf_op jit(solution)/shard_map/reduce_sum | solution.py:46
  139.7 0.3 copy-done.3
  140.0 2.5 %divide_subtract_fusion = f32[2048,400]{0,1:T(8,128)} fusion(f32[2048,400]{0,1:T(8,128)S(1)} %copy-done.3, f32[2048,400]{0,1:T(8,128)S(1)} %get-tuple-element.13, f32[2048]{0:T(1024)S(1)} %sqrt_add_fusion), kind=kLoop, calls=%fused_computation.13 | loop fusion | flops 2457600 | bytes 9838592 | tf_op jit(solution)/shard_map/sub | solution.py:47
  (24 shorter events, 0.1 us)
Async XLA Ops:
  0.6 16.4 %copy-start.12 = (s32[384]{0:T(512)S(1)}, s32[384]{0:T(512)}, u32[]{:S(2)}) copy-start(s32[384]{0:T(512)} %param.10) | copy-start | bytes 4612
  0.6 16.4 %copy-start.2 = (f32[2048,400]{0,1:T(8,128)S(1)}, f32[2048,400]{0,1:T(8,128)}, u32[]{:S(2)}) copy-start(f32[2048,400]{0,1:T(8,128)} %param.8) | copy-start | bytes 9830404
  4.8 18.0 %all-to-all-start = ((s32[16,1,48]{2,1,0:T(1,128)}), s32[16,1,48]{2,1,0:T(1,128)S(1)}, u32[]{:S(2)}, u32[]{:S(2)}) async-start(s32[16,1,48]{2,1,0:T(1,128)} %sub.28), calls=%async_computation | async-start | bytes 16384 | tf_op jit(solution)/shard_map/all_to_all | solution.py:77
  12.9 9.8 %collective-permute-start.3 = (s32[448]{0:T(512)S(1)}, s32[448]{0:T(512)S(1)}, u32[]{:S(2)}, u32[]{:S(2)}) collective-permute-start(s32[448]{0:T(512)S(1)} %pad_add_fusion.2), channel_id=1, source_target_pairs={{0,1},{1,0},{2,3},{3,2},{4,5},{5,4},{6,7},{7,6},{8,9},{9,8},{10,11... | collective-permute-start | bytes 5384 | tf_op jit(solution)/shard_map/ppermute | solution.py:71
  17.0 1.1 copy-start.9
  17.0 1.1 copy-start.11
  18.1 2.5 %copy-start.6 = (f32[384,400]{1,0:T(8,128)}, f32[384,400]{1,0:T(8,128)S(1)}, u32[]{:S(2)}) copy-start(f32[384,400]{1,0:T(8,128)S(1)} %fusion.19) | copy-start | bytes 1843204
  18.6 0.9 copy-start.4
  19.5 3.2 %copy-start.13 = (s32[1,64]{1,0:T(1,128)S(1)}, s32[1,64]{1,0:T(1,128)}, u32[]{:S(2)}) copy-start(s32[1,64]{1,0:T(1,128)} %param.14) | copy-start | bytes 772
  24.1 107.5 %collective-permute-start = (s32[768]{0:T(1024)S(1)}, s32[768]{0:T(1024)S(1)}, u32[]{:S(2)}, u32[]{:S(2)}) collective-permute-start(s32[768]{0:T(1024)S(1)} %reshape.94), channel_id=1, source_target_pairs={{0,1},{1,0},{2,3},{3,2},{4,5},{5,4},{6,7},{7,6},{8,9},{9,8},{10,11... | collective-permute-start | bytes 9224 | tf_op jit(solution)/shard_map/ppermute | solution.py:71
  28.3 0.8 copy-start.8
  74.3 0.9 copy-start
  75.1 3.6 %copy-start.1 = (bf16[16,48,400]{2,1,0:T(8,128)(2,1)S(1)}, bf16[16,48,400]{2,1,0:T(8,128)(2,1)}, u32[]{:S(2)}) copy-start(bf16[16,48,400]{2,1,0:T(8,128)(2,1)} %copy-done) | copy-start | bytes 1843204
  76.7 55.0 %collective-permute-start.2 = (bf16[768,400]{0,1:T(8,128)(2,1)S(1)}, bf16[768,400]{0,1:T(8,128)(2,1)S(1)}, u32[]{:S(2)}, u32[]{:S(2)}) collective-permute-start(bf16[768,400]{0,1:T(8,128)(2,1)S(1)} %copy.36), channel_id=1, source_target_pairs={{0,1},{1,0},{2,3},{3,2},{4,5},{5,4},{6,7},{7,6},{8,9},{9,8},{10,11... | collective-permute-start | bytes 1843208 | tf_op jit(solution)/shard_map/ppermute | solution.py:71
  78.2 53.4 %collective-permute-start.1 = (f32[768]{0:T(1024)S(1)}, f32[768]{0:T(1024)S(1)}, u32[]{:S(2)}, u32[]{:S(2)}) collective-permute-start(f32[768]{0:T(1024)S(1)} %divide_negate_fusion), channel_id=1, source_target_pairs={{0,1},{1,0},{2,3},{3,2},{4,5},{5,4},{6,7},{7,6},{8,9},{9,8},{10,11... | collective-permute-start | bytes 9224 | tf_op jit(solution)/shard_map/ppermute | solution.py:71
  84.0 1.1 copy-start.5
  84.1 1.4 copy-start.7
  126.7 4.2 %copy-start.10 = (f32[64,400]{1,0:T(8,128)S(1)}, f32[64,400]{1,0:T(8,128)}, u32[]{:S(2)}) copy-start(f32[64,400]{1,0:T(8,128)} %param.9) | copy-start | bytes 307204
  138.1 1.9 %copy-start.3 = (f32[2048,400]{0,1:T(8,128)S(1)}, f32[2048,400]{0,1:T(8,128)}, u32[]{:S(2)}) copy-start(f32[2048,400]{0,1:T(8,128)} %param.8) | copy-start | bytes 9830404
